TPU v7x, 32 devices: a whole 2x2x4 slice. The times are simulated.
32 devices in a mesh: groups: 2 (over y), wide: 4 (over z), narrow: 2 (over x), sub: 2 (over core).
Axes of the slice: x: 2, y: 2, z: 4, core: 2. Of those that a mesh axis runs over, the one named last changes fastest.
Arguments:
- state_vel: float32 [2, 512, 512], P(None, ('groups', 'wide'), 'narrow'), parts along dimension 1, may hold values from -6 to 6
- friction: float32 [512, 512], P(('groups', 'wide'), 'narrow'), parts along dimension 0, may hold values from -3 to 3
- basal_area: float32 [512, 512], P(('groups', 'wide'), 'narrow'), parts along dimension 0, may hold values from 0.5 to 2
- direction_beta: float32 [512, 512], P(('groups', 'wide'), 'narrow'), parts along dimension 0, may hold values from -6 to 6
- elem_nodes: int32 [3, 196608], P(None, ('groups', 'wide', 'narrow', 'sub')), parts along dimension 1, may hold values from 0 to 17027
- elem_geom: float32 [7, 196608], P(None, ('groups', 'wide', 'narrow', 'sub')), parts along dimension 1, as said below
- elem_thick: float32 [196608], P(('groups', 'wide', 'narrow', 'sub')), parts along dimension 0, may hold values from 0.3 to 3
- live_blocks: int32 [32], P(('groups', 'wide', 'narrow')), parts along dimension 0, may hold values from 16 to 48, as said below
- pix_dest: int32 [65536, 1], P(('groups', 'wide', 'narrow', 'sub')), parts along dimension 0, may hold values from 0 to 7; in each aligned block of 2048 rows (0 to 2047, 2048 to 4095, ...) at most 512 rows name the same one
- pix_prec: float32 [65536], P(('groups', 'wide', 'narrow', 'sub')), parts along dimension 0, may hold values from 1 to 10
- pix_couple: float32 [65536], P(('groups', 'wide', 'narrow', 'sub')), parts along dimension 0, may hold values from 0 to 0.45
- obs_nodes: int32 [3, 131072], P(None, ('groups', 'wide', 'narrow', 'sub')), parts along dimension 1, may hold values from 0 to 17027
- obs_bary: float32 [3, 131072], P(None, ('groups', 'wide', 'narrow', 'sub')), parts along dimension 1, may hold values from 0 to 1
- obs_angle: float32 [131072], P(('groups', 'wide', 'narrow', 'sub')), parts along dimension 0, may hold values from -3.140625 to 3.140625
Outputs:
- tangent_vel: float32 [2, 512, 512], P(None, ('groups', 'wide'), 'narrow'), parts along dimension 1
- hess_vec: float32 [512, 512], P(('groups', 'wide'), 'narrow'), parts along dimension 0
There are 2 independent parts, one for each index of `groups`. A program takes and returns all parts, laid end to end along the dimension named above; each array names one. Nothing has to cross between parts.
Inputs may be any that keep to these rules, and one draw needn't show every extreme that they name: `live_blocks`: each device's live blocks are its first ones; the two cores of a partition hold at most 64 live blocks together; both bounds are reached. `pix_dest`: at most 512 pixels of one device have the same owner, reached. `elem_nodes`: index into the partition's node grid padded by one row and column on each side, row-major over (66) x (258). `obs_nodes`: as elem_nodes, in the owner partition. `elem_geom`: the three gradients of each direction sum to zero; the area is positive.
All inputs are finite; a program needn't handle non-finite values.
Results may differ from a plain program's by a relative error of at most 0.0003.
Values sent between devices are 32-bit elements; how exact they have to be, the bound alone decides.
A program may use at most 128 MiB of HBM per device.

v0:
```python
import jax
import jax.numpy as jnp
from jax import lax
from jax.sharding import PartitionSpec as P

CG_ITERS = 2


GLEN_B = 1.0
STRAIN_FLOOR = 0.01


def padded(block, sides, width):
    for axis, dim in sides:
        count = lax.axis_size(axis)
        forward = [(i, i + 1) for i in range(count - 1)]
        backward = [(target, source) for source, target in forward]
        low = lax.ppermute(
            lax.slice_in_dim(block, block.shape[dim] - width, None, axis=dim), axis, forward
        )
        high = lax.ppermute(lax.slice_in_dim(block, 0, width, axis=dim), axis, backward)
        block = jnp.concatenate([low, block, high], axis=dim)
    return block


def from_partner(block, axis, bit):
    count = lax.axis_size(axis)
    route = []
    for low in range(count):
        high = low | 1 << bit
        if high != low and high < count:
            route += [(low, high), (high, low)]
    return lax.ppermute(block, axis, route)


def strains(values, geometry):
    strain_xx = jnp.sum(geometry[0:3] * values[0], axis=0)
    strain_yy = jnp.sum(geometry[3:6] * values[1], axis=0)
    strain_xy = 0.5 * jnp.sum(geometry[3:6] * values[0] + geometry[0:3] * values[1], axis=0)
    return (strain_xx, strain_yy, strain_xy)


def forces(values, geometry, coefficient):
    strain_xx, strain_yy, strain_xy = strains(values, geometry)
    stress_xx = coefficient * (2.0 * strain_xx + strain_yy)
    stress_yy = coefficient * (strain_xx + 2.0 * strain_yy)
    stress_xy = coefficient * strain_xy
    force_x = stress_xx * geometry[0:3] + stress_xy * geometry[3:6]
    force_y = stress_yy * geometry[3:6] + stress_xy * geometry[0:3]
    return (force_x, force_y)


def weigh_rows(readings, precision, couple):
    grid_read = readings.reshape(-1, 128)
    grid_prec = precision.reshape(-1, 128)
    grid_couple = couple.reshape(-1, 128)
    column = jnp.arange(128)[None, :]
    next_prec = jnp.concatenate([grid_prec[:, 1:], grid_prec[:, :1]], axis=1)
    link_weight = jnp.where(column < 127, grid_couple * jnp.sqrt(grid_prec * next_prec), 0.0)
    zero_col = jnp.zeros_like(grid_read[:, :1])
    next_read = jnp.concatenate([grid_read[:, 1:], zero_col], axis=1)
    prev_read = jnp.concatenate([zero_col, grid_read[:, :-1]], axis=1)
    prev_link = jnp.concatenate([zero_col, link_weight[:, :-1]], axis=1)
    return (grid_prec * grid_read - link_weight * next_read - prev_link * prev_read).reshape(-1)


def ghosted(field):
    return padded(field, (("wide", 1), ("narrow", 2)), 1)


def core_sum(force_x, force_y, targets, node_rows, columns):
    flat_ids = targets.reshape(-1)
    padded_count = (node_rows + 2) * (columns + 2)
    local_x = jax.ops.segment_sum(force_x.reshape(-1), flat_ids, padded_count)
    local_y = jax.ops.segment_sum(force_y.reshape(-1), flat_ids, padded_count)
    return lax.psum(jnp.stack([local_x, local_y]), "sub").reshape(2, node_rows + 2, columns + 2)


def reduce_rims(summed):
    side_cols = jnp.concatenate([summed[:, :, :1], summed[:, :, -1:]], axis=2)
    beside = padded(side_cols, (("narrow", 2),), 1)
    middle = summed[:, :, 1:-1]
    middle = middle.at[:, :, 0].add(beside[:, :, 0]).at[:, :, -1].add(beside[:, :, 3])
    side_rows = jnp.concatenate([middle[:, :1], middle[:, -1:]], axis=1)
    across = padded(side_rows, (("wide", 1),), 1)
    interior = middle[:, 1:-1]
    return interior.at[:, 0].add(across[:, 0]).at[:, -1].add(across[:, 3])


def norm_sum(residual):
    return lax.psum(jnp.sum(residual * residual), ("wide", "narrow"))


def per_device(
    state_vel,
    friction,
    basal_area,
    direction_beta,
    elem_nodes,
    elem_geom,
    elem_thick,
    live_blocks,
    pix_dest,
    pix_prec,
    pix_couple,
    obs_nodes,
    obs_bary,
    obs_angle,
):
    node_rows, columns = friction.shape
    padded_count = (node_rows + 2) * (columns + 2)
    blocks = elem_nodes.shape[1] // 128
    core_index = lax.axis_index("sub")
    packed = jnp.concatenate([elem_geom, elem_thick[None, :]], axis=0)
    partner_ids = from_partner(elem_nodes, "sub", 0)
    partner_packed = from_partner(packed, "sub", 0)
    first_ids = jnp.where(core_index == 0, elem_nodes, partner_ids).reshape(3, blocks, 128)
    second_ids = jnp.where(core_index == 0, partner_ids, elem_nodes).reshape(3, blocks, 128)
    first_data = jnp.where(core_index == 0, packed, partner_packed).reshape(8, blocks, 128)
    second_data = jnp.where(core_index == 0, partner_packed, packed).reshape(8, blocks, 128)
    share_blocks = 2 * blocks // 3
    position = core_index * share_blocks + jnp.arange(share_blocks, dtype=jnp.int32)
    first_live = live_blocks[0]
    second_live = live_blocks[1]
    from_first = (position < first_live)[None, :, None]
    first_pick = jnp.minimum(position, blocks - 1)
    second_pick = jnp.clip(position - first_live, 0, blocks - 1)
    vertex_ids = jnp.where(
        from_first, first_ids[:, first_pick], second_ids[:, second_pick]
    ).reshape(3, share_blocks * 128)
    element_data = jnp.where(
        from_first, first_data[:, first_pick], second_data[:, second_pick]
    ).reshape(8, share_blocks * 128)
    alive = position < first_live + second_live
    block_mask = jnp.repeat(alive.astype(jnp.float32), 128)
    geometry = element_data[0:7]
    thickness = element_data[7]
    basal_drag = jnp.exp(friction) * basal_area

    def spread(field):
        return ghosted(field).reshape(2, padded_count)

    def finish(force_x, force_y, targets):
        return reduce_rims(core_sum(force_x, force_y, targets, node_rows, columns))

    state_values = spread(state_vel)[:, vertex_ids]
    strain_xx, strain_yy, strain_xy = strains(state_values, geometry)
    effective = (
        strain_xx * strain_xx
        + strain_yy * strain_yy
        + strain_xx * strain_yy
        + strain_xy * strain_xy
        + STRAIN_FLOOR
    )
    viscosity = 0.5 * GLEN_B * effective ** (-1.0 / 3.0)
    coefficient = 2.0 * viscosity * thickness * geometry[6] * block_mask

    def operate(field):
        values = spread(field)[:, vertex_ids]
        force_x, force_y = forces(values, geometry, coefficient)
        return finish(force_x, force_y, vertex_ids) + basal_drag * field

    def solve_field(right_side):
        solution = jnp.zeros_like(right_side)
        residual = right_side
        direction = right_side
        norm_now = norm_sum(residual)
        for iteration in range(CG_ITERS):
            applied = operate(direction)
            step_size = norm_now / lax.psum(jnp.sum(direction * applied), ("wide", "narrow"))
            solution = solution + step_size * direction
            residual = residual - step_size * applied
            if iteration + 1 < CG_ITERS:
                norm_next = norm_sum(residual)
                direction = residual + norm_next / norm_now * direction
                norm_now = norm_next
        return solution

    owners = lax.axis_size(("wide", "narrow"))
    capacity = obs_angle.shape[0] // owners
    tangent_vel = solve_field(-basal_drag * direction_beta * state_vel)
    cosine = jnp.cos(obs_angle)
    sine = jnp.sin(obs_angle)
    picked = spread(tangent_vel)[:, obs_nodes]
    readings = jnp.sum(obs_bary * (cosine * picked[0] + sine * picked[1]), axis=0).reshape(
        owners, capacity
    )
    returned = lax.all_to_all(readings, ("wide", "narrow"), split_axis=0, concat_axis=0, tiled=True)
    target = pix_dest[:, 0]
    onehot = (target[:, None] == jnp.arange(owners, dtype=jnp.int32)[None, :]).astype(jnp.int32)
    running = jnp.cumsum(onehot, axis=0, dtype=jnp.int32)
    slot_rank = jnp.take_along_axis(running, target[:, None], axis=1)[:, 0] - 1
    slot_index = target * capacity + slot_rank
    weighted = weigh_rows(returned.reshape(-1)[slot_index], pix_prec, pix_couple)
    outgoing = (
        jnp.zeros((owners * capacity,), jnp.float32)
        .at[slot_index]
        .set(weighted)
        .reshape(owners, capacity)
    )
    arrived = lax.all_to_all(outgoing, ("wide", "narrow"), split_axis=0, concat_axis=0, tiled=True)
    arrived = arrived.reshape(-1)
    adjoint_rhs = finish(obs_bary * arrived * cosine, obs_bary * arrived * sine, obs_nodes)
    adjoint = solve_field(adjoint_rhs)
    hess_vec = -basal_drag * (state_vel[0] * adjoint[0] + state_vel[1] * adjoint[1])
    return (tangent_vel, hess_vec)


def solution(mesh):
    placed = (
        P(None, ("groups", "wide"), "narrow"),
        P(("groups", "wide"), "narrow"),
        P(("groups", "wide"), "narrow"),
        P(("groups", "wide"), "narrow"),
        P(None, ("groups", "wide", "narrow", "sub")),
        P(None, ("groups", "wide", "narrow", "sub")),
        P(("groups", "wide", "narrow", "sub")),
        P(("groups", "wide", "narrow")),
        P(("groups", "wide", "narrow", "sub"), None),
        P(("groups", "wide", "narrow", "sub")),
        P(("groups", "wide", "narrow", "sub")),
        P(None, ("groups", "wide", "narrow", "sub")),
        P(None, ("groups", "wide", "narrow", "sub")),
        P(("groups", "wide", "narrow", "sub")),
    )
    return jax.shard_map(
        per_device,
        mesh=mesh,
        in_specs=placed,
        out_specs=(P(None, ("groups", "wide"), "narrow"), P(("groups", "wide"), "narrow")),
        check_vma=False,
    )
```

profile of v0, /device:TPU:0, one launch (start us, length us, event | category | flops | bytes accessed | tf_op | source)
XLA Modules:
  0.0 1470.3 jit_solution(11288012190379381015)
XLA Ops:
  57.0 44.6 %gather_fusion.4 = f32[12288,2]{1,0:T(8,128)} fusion(f32[2,17028]{0,1:T(8,128)} %copy.93, s32[12288]{0:T(1024)S(1)} %broadcast_clamp_fusion.1), kind=kCustom, calls=%fused_computation.4 | custom fusion | bytes 245760 | tf_op jit(solution)/shard_map/gather | solution.py:146
  106.6 44.9 %gather_fusion.5 = f32[12288,2]{1,0:T(8,128)} fusion(f32[2,17028]{0,1:T(8,128)} %copy.95, s32[12288]{0:T(1024)S(1)} %broadcast_clamp_fusion.1), kind=kCustom, calls=%fused_computation.5 | custom fusion | bytes 245760 | tf_op jit(solution)/shard_map/gather | solution.py:159
  158.1 64.5 %scatter_custom_fusion = f32[17028]{0:T(1024)S(1)} fusion(s32[12288]{0:T(1024)S(1)} %bitcast.330, f32[12288]{0:T(1024)S(1)} %get-tuple-element.310, f32[]{:T(128)} %constant.466.clone.1), kind=kCustom, calls=%fused_computation.177 | custom fusion | flops 12288 | bytes 68116 | tf_op jit(solution)/shard_map/scatter-add | solution.py:74
  222.7 64.5 %scatter_custom_fusion.1 = f32[17028]{0:T(1024)S(1)} fusion(s32[12288]{0:T(1024)S(1)} %bitcast.331, f32[12288]{0:T(1024)S(1)} %get-tuple-element.311, f32[]{:T(128)} %constant.466.clone.1), kind=kCustom, calls=%fused_computation.175 | custom fusion | flops 12288 | bytes 68116 | tf_op jit(solution)/shard_map/scatter-add | solution.py:75
  288.4 19.4 %all-reduce.11.cloned.1.call-done = f32[2,66,258]{2,1,0:T(8,128)} async-done(((f32[2,66,258]{2,1,0:T(8,128)}), f32[2,66,258]{2,1,0:T(8,128)}) %all-reduce.11.cloned.1.call-update) | async-done | bytes 136240 | tf_op jit(solution)/shard_map/psum | solution.py:76
  328.9 18.7 %all-reduce.4 = (f32[]{:T(128)}, f32[]{:T(128)}) all-reduce(f32[]{:T(128)} %get-tuple-element.260, f32[]{:T(128)} %get-tuple-element.259), channel_id=1, replica_groups=mesh['groups'=2,'wide'=4,'narrow'=2,'sub'=2] {'wide','narrow'}, use_global_device_ids=true, to_apply=%region_1.2 | all-reduce | flops 2 | bytes 16 | tf_op jit(solution)/shard_map/psum | solution.py:91
  349.6 18.8 %psum.94 = f32[]{:T(128)} all-reduce(f32[]{:T(128)} %multiply_reduce_fusion.5), channel_id=1, replica_groups=mesh['groups'=2,'wide'=4,'narrow'=2,'sub'=2] {'wide','narrow'}, use_global_device_ids=true, to_apply=%region_14.15 | all-reduce | flops 1 | bytes 8 | tf_op jit(solution)/shard_map/psum | solution.py:91
  391.4 44.8 %gather_fusion.6 = f32[12288,2]{1,0:T(8,128)} fusion(f32[2,17028]{0,1:T(8,128)} %copy.97, s32[12288]{0:T(1024)S(1)} %broadcast_clamp_fusion.1), kind=kCustom, calls=%fused_computation.6 | custom fusion | bytes 245760 | tf_op jit(solution)/shard_map/gather | solution.py:159
  441.4 64.5 %scatter_custom_fusion.2 = f32[17028]{0:T(1024)S(1)} fusion(s32[12288]{0:T(1024)S(1)} %bitcast.332, f32[12288]{0:T(1024)S(1)} %get-tuple-element.304, f32[]{:T(128)} %constant.466.clone.1), kind=kCustom, calls=%fused_computation.173 | custom fusion | flops 12288 | bytes 68116 | tf_op jit(solution)/shard_map/scatter-add | solution.py:74
  506.0 64.5 %scatter_custom_fusion.3 = f32[17028]{0:T(1024)S(1)} fusion(s32[12288]{0:T(1024)S(1)} %bitcast.333, f32[12288]{0:T(1024)S(1)} %get-tuple-element.305, f32[]{:T(128)} %constant.466.clone.1), kind=kCustom, calls=%fused_computation.171 | custom fusion | flops 12288 | bytes 68116 | tf_op jit(solution)/shard_map/scatter-add | solution.py:75
  574.4 13.9 all-reduce.13.cloned.1.call-done
  593.2 12.5 gather_fusion.11
  622.1 18.4 %psum.96 = f32[]{:T(128)} all-reduce(f32[]{:T(128)} %multiply_reduce_fusion.4), channel_id=1, replica_groups=mesh['groups'=2,'wide'=4,'narrow'=2,'sub'=2] {'wide','narrow'}, use_global_device_ids=true, to_apply=%region_22.23 | all-reduce | flops 1 | bytes 8 | tf_op jit(solution)/shard_map/psum | solution.py:170
  663.9 44.8 %gather_fusion.7 = f32[12288,2]{1,0:T(8,128)} fusion(f32[2,17028]{0,1:T(8,128)} %copy.99, s32[12288]{0:T(1024)S(1)} %broadcast_clamp_fusion), kind=kCustom, calls=%fused_computation.7 | custom fusion | bytes 245760 | tf_op jit(solution)/shard_map/gather | solution.py:184
  717.7 6.5 all-to-all-done
  724.2 11.8 gather_fusion.8
  736.1 8.6 scatter_custom_fusion.4
  748.2 6.4 all-to-all-done.1
  754.7 64.7 %scatter_custom_fusion.5 = f32[17028]{0:T(1024)S(1)} fusion(s32[12288]{0:T(1024)S(1)} %reshape.1519, f32[12288]{0:T(1024)S(1)} %reshape.1521, f32[]{:T(128)} %constant.466.clone.1), kind=kCustom, calls=%fused_computation.169 | custom fusion | flops 12288 | bytes 68116 | tf_op jit(solution)/shard_map/scatter-add | solution.py:74
  819.5 64.5 %scatter_custom_fusion.6 = f32[17028]{0:T(1024)S(1)} fusion(s32[12288]{0:T(1024)S(1)} %reshape.1519, f32[12288]{0:T(1024)S(1)} %reshape.1529, f32[]{:T(128)} %constant.466.clone.1), kind=kCustom, calls=%fused_computation.167 | custom fusion | flops 12288 | bytes 68116 | tf_op jit(solution)/shard_map/scatter-add | solution.py:75
  885.2 15.5 %all-reduce.15.cloned.1.call-done = f32[2,66,258]{2,1,0:T(8,128)} async-done(((f32[2,66,258]{2,1,0:T(8,128)}), f32[2,66,258]{2,1,0:T(8,128)}) %all-reduce.15.cloned.1.call-update) | async-done | bytes 136240 | tf_op jit(solution)/shard_map/psum | solution.py:76
  941.9 44.8 %gather_fusion.9 = f32[12288,2]{1,0:T(8,128)} fusion(f32[2,17028]{0,1:T(8,128)} %copy.101, s32[12288]{0:T(1024)S(1)} %broadcast_clamp_fusion.1), kind=kCustom, calls=%fused_computation.9 | custom fusion | bytes 245760 | tf_op jit(solution)/shard_map/gather | solution.py:159
  991.9 64.5 %scatter_custom_fusion.7 = f32[17028]{0:T(1024)S(1)} fusion(s32[12288]{0:T(1024)S(1)} %bitcast.334, f32[12288]{0:T(1024)S(1)} %get-tuple-element.294, f32[]{:T(128)} %constant.466.clone.1), kind=kCustom, calls=%fused_computation.165 | custom fusion | flops 12288 | bytes 68116 | tf_op jit(solution)/shard_map/scatter-add | solution.py:74
  1056.5 64.5 %scatter_custom_fusion.8 = f32[17028]{0:T(1024)S(1)} fusion(s32[12288]{0:T(1024)S(1)} %bitcast.335, f32[12288]{0:T(1024)S(1)} %get-tuple-element.295, f32[]{:T(128)} %constant.466.clone.1), kind=kCustom, calls=%fused_computation.163 | custom fusion | flops 12288 | bytes 68116 | tf_op jit(solution)/shard_map/scatter-add | solution.py:75
  1122.1 19.0 %all-reduce.17.cloned.1.call-done = f32[2,66,258]{2,1,0:T(8,128)} async-done(((f32[2,66,258]{2,1,0:T(8,128)}), f32[2,66,258]{2,1,0:T(8,128)}) %all-reduce.17.cloned.1.call-update) | async-done | bytes 136240 | tf_op jit(solution)/shard_map/psum | solution.py:76
  1162.2 18.7 %all-reduce.3 = (f32[]{:T(128)}, f32[]{:T(128)}) all-reduce(f32[]{:T(128)} %get-tuple-element.258, f32[]{:T(128)} %get-tuple-element.257), channel_id=1, replica_groups=mesh['groups'=2,'wide'=4,'narrow'=2,'sub'=2] {'wide','narrow'}, use_global_device_ids=true, to_apply=%region_31.32 | all-reduce | flops 2 | bytes 16 | tf_op jit(solution)/shard_map/psum | solution.py:91
  1182.8 18.8 %psum.101 = f32[]{:T(128)} all-reduce(f32[]{:T(128)} %multiply_reduce_fusion.1), channel_id=1, replica_groups=mesh['groups'=2,'wide'=4,'narrow'=2,'sub'=2] {'wide','narrow'}, use_global_device_ids=true, to_apply=%region_41.42 | all-reduce | flops 1 | bytes 8 | tf_op jit(solution)/shard_map/psum | solution.py:91
  1224.5 44.8 %gather_fusion.10 = f32[12288,2]{1,0:T(8,128)} fusion(f32[2,17028]{0,1:T(8,128)} %copy.103, s32[12288]{0:T(1024)S(1)} %broadcast_clamp_fusion.1), kind=kCustom, calls=%fused_computation.10 | custom fusion | bytes 245760 | tf_op jit(solution)/shard_map/gather | solution.py:159
  1274.5 64.5 %scatter_custom_fusion.9 = f32[17028]{0:T(1024)S(1)} fusion(s32[12288]{0:T(1024)S(1)} %bitcast.336, f32[12288]{0:T(1024)S(1)} %get-tuple-element.288, f32[]{:T(128)} %constant.466.clone.1), kind=kCustom, calls=%fused_computation.161 | custom fusion | flops 12288 | bytes 68116 | tf_op jit(solution)/shard_map/scatter-add | solution.py:74
  1339.0 64.5 %scatter_custom_fusion.10 = f32[17028]{0:T(1024)S(1)} fusion(s32[12288]{0:T(1024)S(1)} %bitcast.337, f32[12288]{0:T(1024)S(1)} %get-tuple-element.289, f32[]{:T(128)} %constant.466.clone.1), kind=kCustom, calls=%fused_computation.159 | custom fusion | flops 12288 | bytes 68116 | tf_op jit(solution)/shard_map/scatter-add | solution.py:75
  1404.7 16.7 %all-reduce.19.cloned.1.call-done = f32[2,66,258]{2,1,0:T(8,128)} async-done(((f32[2,66,258]{2,1,0:T(8,128)}), f32[2,66,258]{2,1,0:T(8,128)}) %all-reduce.19.cloned.1.call-update) | async-done | bytes 136240 | tf_op jit(solution)/shard_map/psum | solution.py:76
  1442.5 18.8 %psum.103 = f32[]{:T(128)} all-reduce(f32[]{:T(128)} %multiply_reduce_fusion), channel_id=1, replica_groups=mesh['groups'=2,'wide'=4,'narrow'=2,'sub'=2] {'wide','narrow'}, use_global_device_ids=true, to_apply=%region_49.50 | all-reduce | flops 1 | bytes 8 | tf_op jit(solution)/shard_map/psum | solution.py:170
  (350 shorter events, 288.4 us)
Async XLA Ops:
  7.2 300.6 %all-reduce.11.cloned.1.call-start = ((), (), s32[]{:S(2)}) async-start(), calls=%async_computation.2 | async-start | bytes 442368 | tf_op jit(solution)/shard_map/psum | solution.py:76
  8.0 22.9 %collective-permute-start.2 = (f32[2,1,256]{2,1,0:T(1,128)S(1)}, f32[2,1,256]{2,1,0:T(1,128)S(1)}, u32[]{:S(2)}, u32[]{:S(2)}) collective-permute-start(f32[2,1,256]{2,1,0:T(1,128)S(1)} %get-tuple-element.332), channel_id=1, source_target_pairs={{0,4},{4,8},{8,12},{1,5},{5,9},{9,13},{2,6},{6,10},{10,14},{3,7},{... | collective-permute-start | bytes 6152 | tf_op jit(solution)/shard_map/ppermute | solution.py:18
  12.9 19.2 %collective-permute-start.3 = (f32[2,1,256]{2,1,0:T(1,128)S(1)}, f32[2,1,256]{2,1,0:T(1,128)S(1)}, u32[]{:S(2)}, u32[]{:S(2)}) collective-permute-start(f32[2,1,256]{2,1,0:T(1,128)S(1)} %get-tuple-element.333), channel_id=1, source_target_pairs={{4,0},{8,4},{12,8},{5,1},{9,5},{13,9},{6,2},{10,6},{14,10},{7,3},{... | collective-permute-start | bytes 6152 | tf_op jit(solution)/shard_map/ppermute | solution.py:21
  14.2 41.3 %collective-permute-start = (s32[3,6144]{1,0:T(4,128)}, s32[3,6144]{1,0:T(4,128)S(1)}, u32[]{:S(2)}, u32[]{:S(2)}) collective-permute-start(s32[3,6144]{1,0:T(4,128)} %param.58), channel_id=1, source_target_pairs={{0,1},{1,0},{2,3},{3,2},{4,5},{5,4},{6,7},{7,6},{8,9},{9,8},{10,11... | collective-permute-start | bytes 221192 | tf_op jit(solution)/shard_map/ppermute | solution.py:33
  16.1 10.9 collective-permute-start.6
  20.7 6.6 collective-permute-start.7
  27.0 129.4 %collective-permute-start.1 = (f32[8,6144]{1,0:T(8,128)S(1)}, f32[8,6144]{1,0:T(8,128)S(1)}, u32[]{:S(2)}, u32[]{:S(2)}) collective-permute-start(f32[8,6144]{1,0:T(8,128)S(1)} %pad_maximum_fusion.6), channel_id=1, source_target_pairs={{0,1},{1,0},{2,3},{3,2},{4,5},{5,4},{6,7},{7,6},{8,9},{9,8},{10,11... | collective-permute-start | bytes 589832 | tf_op jit(solution)/shard_map/ppermute | solution.py:33
  27.4 10.3 collective-permute-start.8
  30.8 8.2 collective-permute-start.9
  33.1 6.5 collective-permute-start.4
  37.7 6.2 collective-permute-start.5
  288.3 300.0 %all-reduce.13.cloned.1.call-start = ((), (), s32[]{:S(2)}) async-start(), calls=%async_computation.3 | async-start | bytes 442368 | tf_op jit(solution)/shard_map/psum | solution.py:76
  308.8 6.1 collective-permute-start.10
  312.5 6.2 collective-permute-start.11
  379.6 6.2 collective-permute-start.17
  589.4 17.7 %collective-permute-start.18 = (f32[2,66,1]{2,1,0:T(8,128)S(1)}, f32[2,66,1]{2,1,0:T(8,128)S(1)}, u32[]{:S(2)}, u32[]{:S(2)}) collective-permute-start(f32[2,66,1]{2,1,0:T(8,128)S(1)} %get-tuple-element.281), channel_id=1, source_target_pairs={{0,2},{1,3},{4,6},{5,7},{8,10},{9,11},{12,14},{13,15},{16,18},{17,... | collective-permute-start | bytes 1592 | tf_op jit(solution)/shard_map/ppermute | solution.py:18
  605.7 6.2 collective-permute-start.19
  652.1 6.2 collective-permute-start.25
  714.3 9.9 all-to-all-start
  744.7 9.9 all-to-all-start.1
  748.1 152.6 %all-reduce.15.cloned.1.call-start = ((), (), s32[]{:S(2)}) async-start(), calls=%async_computation.4 | async-start | bytes 442368 | tf_op jit(solution)/shard_map/psum | solution.py:76
  885.1 256.0 %all-reduce.17.cloned.1.call-start = ((), (), s32[]{:S(2)}) async-start(), calls=%async_computation.5 | async-start | bytes 442368 | tf_op jit(solution)/shard_map/psum | solution.py:76
  901.6 6.0 collective-permute-start.26
  905.3 6.2 collective-permute-start.27
  921.0 5.9 collective-permute-start.31
  930.1 6.2 collective-permute-start.33
  1122.1 299.3 %all-reduce.19.cloned.1.call-start = ((), (), s32[]{:S(2)}) async-start(), calls=%async_computation.6 | async-start | bytes 442368 | tf_op jit(solution)/shard_map/psum | solution.py:76
  1142.2 6.0 collective-permute-start.34
  1145.8 6.2 collective-permute-start.35
  1212.7 6.2 collective-permute-start.41
  1422.4 6.0 collective-permute-start.42
  1426.1 6.2 collective-permute-start.43
  (33 other events, 1129.2 us)
Sparse Core Ops, SparseCore 0:
  288.4 19.3 all-reduce.10
  571.7 16.5 all-reduce.12
  885.2 15.3 all-reduce.14
  1122.2 18.8 all-reduce.16
  1404.8 16.5 all-reduce.18
where the time goes:
time: 1480 us; the launch traced here: 1470 us
  other arithmetic  666 us (45%)
  local copies, waits for them, and re-layouts  388 us (26%)
  waiting for transfers between devices  171 us (12%)
  blocking collectives  112 us (8%)
  starting transfers between devices  108 us (7%)
  between operations  25.4 us (2%)
    scatter-add x5, other arithmetic, core_sum(): local_x = jax.ops.segment_sum(force_x.reshape(-1), flat_ids, padded_count)  323 us
    scatter-add x5, other arithmetic, core_sum(): local_y = jax.ops.segment_sum(force_y.reshape(-1), flat_ids, padded_count)  322 us
    gather x8, local copies, waits for them, and re-layouts, operate(): values = spread(field)[:, vertex_ids]  199 us
    psum x5, waiting for transfers between devices, core_sum(): lax.psum(jnp.stack([local_x, local_y]), 'sub')  84.5 us
    psum x4, blocking collectives, norm_sum(): return lax.psum(jnp.sum(residual * residual), ('wide', 'narrow'))  75 us
    ppermute x22, starting transfers between devices, padded(): lax.ppermute(lax.slice_in_dim(block, block.shape[dim] - width, None, axis...  71.9 us
    ppermute x22, waiting for transfers between devices, padded(): lax.ppermute(lax.slice_in_dim(block, 0, width, axis=dim), axis, backward)  69.8 us
    gather x2, local copies, waits for them, and re-layouts, per_device(): picked = spread(tangent_vel)[:, obs_nodes]  49.7 us
  transfers between devices with their start and end apart: 53, of which 31 were waited for; matrix products, arithmetic and copies ran while one was open for 10% of the time, Pallas kernels for 0%

commit v1 on v0

v1 whole, which is shorter than its diff:
```python
import functools

import jax
import jax.numpy as jnp
from jax import lax
from jax.experimental import pallas as pl
from jax.experimental.pallas import tpu as pltpu
from jax.sharding import PartitionSpec as P

CG_ITERS = 2

GLEN_B = 1.0
STRAIN_FLOOR = 0.01
RIM = 128
CHUNK = 512


def padded(block, sides, width):
    for axis, dim in sides:
        count = lax.axis_size(axis)
        forward = [(i, i + 1) for i in range(count - 1)]
        backward = [(target, source) for source, target in forward]
        low = lax.ppermute(
            lax.slice_in_dim(block, block.shape[dim] - width, None, axis=dim), axis, forward
        )
        high = lax.ppermute(lax.slice_in_dim(block, 0, width, axis=dim), axis, backward)
        block = jnp.concatenate([low, block, high], axis=dim)
    return block


def split_pair(values):
    high = values.astype(jnp.bfloat16)
    low = (values - high.astype(jnp.float32)).astype(jnp.bfloat16)
    return high, low


def stack_field(field):
    high_x, low_x = split_pair(field[0])
    high_y, low_y = split_pair(field[1])
    return jnp.concatenate([high_x, high_y, low_x, low_y], axis=0)


def column_onehot(low_ids, width):
    place = lax.broadcasted_iota(jnp.int32, (width, low_ids.shape[1]), 0)
    return jnp.where(place == low_ids, 1.0, 0.0).astype(jnp.bfloat16)


def row_mask(high_ids, rows):
    return lax.broadcasted_iota(jnp.int32, (rows, high_ids.shape[1]), 0) == high_ids


def pick(stacked, mask, onehot):
    rows = mask.shape[0]
    grown = jnp.dot(stacked, onehot, preferred_element_type=jnp.float32)
    both = grown[: 2 * rows] + grown[2 * rows :]
    value_x = jnp.sum(jnp.where(mask, both[:rows], 0.0), axis=0, keepdims=True)
    value_y = jnp.sum(jnp.where(mask, both[rows:], 0.0), axis=0, keepdims=True)
    return value_x, value_y


def masked_stack(mask, value_x, value_y):
    parts = split_f32(value_x, value_y)
    return jnp.concatenate(
        [jnp.where(mask, part, 0.0).astype(jnp.bfloat16) for part in parts], axis=0
    )


def split_f32(value_x, value_y):
    high_x = value_x.astype(jnp.bfloat16).astype(jnp.float32)
    high_y = value_y.astype(jnp.bfloat16).astype(jnp.float32)
    return high_x, high_y, value_x - high_x, value_y - high_y


def add_in(stacks, onehots):
    left = jnp.concatenate(stacks, axis=1)
    right = jnp.concatenate(onehots, axis=1)
    return lax.dot_general(
        left, right, (((1,), (1,)), ((), ())), preferred_element_type=jnp.float32
    )


def unstack(total):
    both = total[: total.shape[0] // 2] + total[total.shape[0] // 2 :]
    rows = both.shape[0] // 2
    return both[:rows], both[rows:]


def strain_rows(values, grad):
    value_x, value_y = values
    strain_xx = grad[0] * value_x[0] + grad[1] * value_x[1] + grad[2] * value_x[2]
    strain_yy = grad[3] * value_y[0] + grad[4] * value_y[1] + grad[5] * value_y[2]
    strain_xy = 0.5 * (
        (grad[3] * value_x[0] + grad[0] * value_y[0])
        + (grad[4] * value_x[1] + grad[1] * value_y[1])
        + (grad[5] * value_x[2] + grad[2] * value_y[2])
    )
    return strain_xx, strain_yy, strain_xy


def chunk_of(step):
    return pl.ds(pl.multiple_of(step * CHUNK, CHUNK), CHUNK)


def gather_chunk(stacked, high_ref, low_ref, cols, rows, width):
    masks, onehots, value_x, value_y = [], [], [], []
    for a in range(3):
        mask = row_mask(high_ref[a : a + 1, cols], rows)
        onehot = column_onehot(low_ref[a : a + 1, cols], width)
        got_x, got_y = pick(stacked, mask, onehot)
        masks.append(mask)
        onehots.append(onehot)
        value_x.append(got_x)
        value_y.append(got_y)
    return masks, onehots, (value_x, value_y)


def viscosity_loop(stack_ref, high_ref, low_ref, geom_ref, scale_ref, coef_ref, rows):
    width = stack_ref.shape[1]

    def body(step, carry):
        cols = chunk_of(step)
        _, _, values = gather_chunk(stack_ref[...], high_ref, low_ref, cols, rows, width)
        grad = [geom_ref[i : i + 1, cols] for i in range(6)]
        exx, eyy, exy = strain_rows(values, grad)
        effective = exx * exx + eyy * eyy + exx * eyy + exy * exy + STRAIN_FLOOR
        viscosity = 0.5 * GLEN_B * jnp.exp(jnp.log(effective) * (-1.0 / 3.0))
        coef_ref[:, cols] = 2.0 * viscosity * scale_ref[:, cols]
        return carry

    lax.fori_loop(0, high_ref.shape[1] // CHUNK, body, 0)


def operate_loop(stack_ref, high_ref, low_ref, geom_ref, coef_ref, total_ref, rows):
    width = stack_ref.shape[1]
    total_ref[...] = jnp.zeros_like(total_ref)

    def body(step, carry):
        cols = chunk_of(step)
        masks, onehots, values = gather_chunk(
            stack_ref[...], high_ref, low_ref, cols, rows, width
        )
        grad = [geom_ref[i : i + 1, cols] for i in range(6)]
        coefficient = coef_ref[:, cols]
        exx, eyy, exy = strain_rows(values, grad)
        sxx = coefficient * (2.0 * exx + eyy)
        syy = coefficient * (exx + 2.0 * eyy)
        sxy = coefficient * exy
        stacks = [
            masked_stack(
                masks[a],
                sxx * grad[a] + sxy * grad[3 + a],
                syy * grad[3 + a] + sxy * grad[a],
            )
            for a in range(3)
        ]
        total_ref[...] += add_in(stacks, onehots)
        return carry

    lax.fori_loop(0, high_ref.shape[1] // CHUNK, body, 0)


def read_loop(stack_ref, high_ref, low_ref, weight_x_ref, weight_y_ref, read_ref, rows):
    width = stack_ref.shape[1]

    def body(step, carry):
        cols = chunk_of(step)
        _, _, values = gather_chunk(stack_ref[...], high_ref, low_ref, cols, rows, width)
        total = 0.0
        for a in range(3):
            total = total + (
                weight_x_ref[a : a + 1, cols] * values[0][a]
                + weight_y_ref[a : a + 1, cols] * values[1][a]
            )
        read_ref[:, cols] = total
        return carry

    lax.fori_loop(0, high_ref.shape[1] // CHUNK, body, 0)


def spread_loop(arrived_ref, high_ref, low_ref, weight_x_ref, weight_y_ref, total_ref, rows):
    width = total_ref.shape[1]
    total_ref[...] = jnp.zeros_like(total_ref)

    def body(step, carry):
        cols = chunk_of(step)
        arrived = arrived_ref[:, cols]
        stacks, onehots = [], []
        for a in range(3):
            mask = row_mask(high_ref[a : a + 1, cols], rows)
            onehots.append(column_onehot(low_ref[a : a + 1, cols], width))
            stacks.append(
                masked_stack(
                    mask,
                    arrived * weight_x_ref[a : a + 1, cols],
                    arrived * weight_y_ref[a : a + 1, cols],
                )
            )
        total_ref[...] += add_in(stacks, onehots)
        return carry

    lax.fori_loop(0, high_ref.shape[1] // CHUNK, body, 0)


def viscosity_kernel(field_ref, high_ref, low_ref, geom_ref, scale_ref, coef_ref, stack_ref):
    stack_ref[...] = stack_field(field_ref)
    viscosity_loop(
        stack_ref, high_ref, low_ref, geom_ref, scale_ref, coef_ref, field_ref.shape[1]
    )


def operate_kernel(
    field_ref, high_ref, low_ref, geom_ref, coef_ref, out_ref, stack_ref, total_ref
):
    stack_ref[...] = stack_field(field_ref)
    operate_loop(
        stack_ref, high_ref, low_ref, geom_ref, coef_ref, total_ref, field_ref.shape[1]
    )
    out_ref[0], out_ref[1] = unstack(total_ref[...])


def read_kernel(field_ref, high_ref, low_ref, wx_ref, wy_ref, read_ref, stack_ref):
    stack_ref[...] = stack_field(field_ref)
    read_loop(stack_ref, high_ref, low_ref, wx_ref, wy_ref, read_ref, field_ref.shape[1])


def spread_kernel(arrived_ref, high_ref, low_ref, wx_ref, wy_ref, out_ref, total_ref):
    spread_loop(arrived_ref, high_ref, low_ref, wx_ref, wy_ref, total_ref, out_ref.shape[1])
    out_ref[0], out_ref[1] = unstack(total_ref[...])


def call(kernel, out, scratch, *args):
    return pl.pallas_call(
        kernel,
        out_shape=jax.ShapeDtypeStruct(out, jnp.float32),
        in_specs=[pl.BlockSpec(memory_space=pltpu.VMEM)] * len(args),
        out_specs=pl.BlockSpec(memory_space=pltpu.VMEM),
        scratch_shapes=scratch,
        compiler_params=pltpu.CompilerParams(vmem_limit_bytes=48 * 1024 * 1024),
    )(*args)


def split_ids(ids, node_rows, columns):
    row = ids // (columns + 2)
    col = ids % (columns + 2)
    left, right = col == 0, col == columns + 1
    high = jnp.where(left | right, node_rows + 2, row)
    low = jnp.where(left, row, jnp.where(right, row + RIM, col - 1))
    return high, low


def weigh_rows(readings, precision, couple):
    grid_read = readings.reshape(-1, 128)
    grid_prec = precision.reshape(-1, 128)
    grid_couple = couple.reshape(-1, 128)
    column = jnp.arange(128)[None, :]
    next_prec = jnp.concatenate([grid_prec[:, 1:], grid_prec[:, :1]], axis=1)
    link_weight = jnp.where(column < 127, grid_couple * jnp.sqrt(grid_prec * next_prec), 0.0)
    zero_col = jnp.zeros_like(grid_read[:, :1])
    next_read = jnp.concatenate([grid_read[:, 1:], zero_col], axis=1)
    prev_read = jnp.concatenate([zero_col, grid_read[:, :-1]], axis=1)
    prev_link = jnp.concatenate([zero_col, link_weight[:, :-1]], axis=1)
    return (grid_prec * grid_read - link_weight * next_read - prev_link * prev_read).reshape(-1)


def ghosted(field):
    return padded(field, (("wide", 1), ("narrow", 2)), 1)


def reduce_rims(summed):
    side_cols = jnp.concatenate([summed[:, :, :1], summed[:, :, -1:]], axis=2)
    beside = padded(side_cols, (("narrow", 2),), 1)
    middle = summed[:, :, 1:-1]
    middle = middle.at[:, :, 0].add(beside[:, :, 0]).at[:, :, -1].add(beside[:, :, 3])
    side_rows = jnp.concatenate([middle[:, :1], middle[:, -1:]], axis=1)
    across = padded(side_rows, (("wide", 1),), 1)
    interior = middle[:, 1:-1]
    return interior.at[:, 0].add(across[:, 0]).at[:, -1].add(across[:, 3])


def norm_sum(residual):
    return lax.psum(jnp.sum(residual * residual), ("wide", "narrow"))


def per_device(
    state_vel,
    friction,
    basal_area,
    direction_beta,
    elem_nodes,
    elem_geom,
    elem_thick,
    live_blocks,
    pix_dest,
    pix_prec,
    pix_couple,
    obs_nodes,
    obs_bary,
    obs_angle,
):
    node_rows, columns = friction.shape
    rows = -(-(node_rows + 3) // 8) * 8
    elements = elem_nodes.shape[1]
    core_index = lax.axis_index("sub")
    alive = jnp.arange(elements, dtype=jnp.int32) // 128 < live_blocks[core_index]
    scale = jnp.where(alive, elem_thick * elem_geom[6], 0.0)[None, :]
    high, low = split_ids(elem_nodes, node_rows, columns)
    obs_high, obs_low = split_ids(obs_nodes, node_rows, columns)
    basal_drag = jnp.exp(friction) * basal_area
    stack = pltpu.VMEM((4 * rows, columns), jnp.bfloat16)
    total = pltpu.VMEM((4 * rows, columns), jnp.float32)

    def spread(field):
        wide = ghosted(field)
        room = ((0, 0), (0, RIM - node_rows - 2))
        rim = jnp.concatenate([jnp.pad(wide[:, :, 0], room), jnp.pad(wide[:, :, -1], room)], axis=1)
        gap = jnp.zeros((2, rows - node_rows - 3, columns), jnp.float32)
        return jnp.concatenate([wide[:, :, 1:-1], rim[:, None, :], gap], axis=1)

    def finish(partial):
        both = lax.psum(partial, "sub")
        rim = both[:, node_rows + 2]
        left = rim[:, : node_rows + 2, None]
        right = rim[:, RIM : RIM + node_rows + 2, None]
        return reduce_rims(jnp.concatenate([left, both[:, : node_rows + 2], right], axis=2))

    coefficient = call(
        viscosity_kernel, (1, elements), [stack], spread(state_vel), high, low, elem_geom, scale
    )

    def operate(field):
        partial = call(
            operate_kernel,
            (2, rows, columns),
            [stack, total],
            spread(field),
            high,
            low,
            elem_geom,
            coefficient,
        )
        return finish(partial) + basal_drag * field

    def solve_field(right_side):
        solution = jnp.zeros_like(right_side)
        residual = right_side
        direction = right_side
        norm_now = norm_sum(residual)
        for iteration in range(CG_ITERS):
            applied = operate(direction)
            step_size = norm_now / lax.psum(jnp.sum(direction * applied), ("wide", "narrow"))
            solution = solution + step_size * direction
            residual = residual - step_size * applied
            if iteration + 1 < CG_ITERS:
                norm_next = norm_sum(residual)
                direction = residual + norm_next / norm_now * direction
                norm_now = norm_next
        return solution

    owners = lax.axis_size(("wide", "narrow"))
    capacity = obs_angle.shape[0] // owners
    tangent_vel = solve_field(-basal_drag * direction_beta * state_vel)
    weight_x = obs_bary * jnp.cos(obs_angle)
    weight_y = obs_bary * jnp.sin(obs_angle)
    readings = call(
        read_kernel,
        (1, obs_angle.shape[0]),
        [stack],
        spread(tangent_vel),
        obs_high,
        obs_low,
        weight_x,
        weight_y,
    ).reshape(owners, capacity)
    returned = lax.all_to_all(readings, ("wide", "narrow"), split_axis=0, concat_axis=0, tiled=True)
    target = pix_dest[:, 0]
    onehot = (target[:, None] == jnp.arange(owners, dtype=jnp.int32)[None, :]).astype(jnp.int32)
    running = jnp.cumsum(onehot, axis=0, dtype=jnp.int32)
    slot_rank = jnp.sum(jnp.where(onehot == 1, running, 0), axis=1) - 1
    slot_index = target * capacity + slot_rank
    weighted = weigh_rows(returned.reshape(-1)[slot_index], pix_prec, pix_couple)
    outgoing = (
        jnp.zeros((owners * capacity,), jnp.float32)
        .at[slot_index]
        .set(weighted)
        .reshape(owners, capacity)
    )
    arrived = lax.all_to_all(outgoing, ("wide", "narrow"), split_axis=0, concat_axis=0, tiled=True)
    partial = call(
        spread_kernel,
        (2, rows, columns),
        [total],
        arrived.reshape(1, -1),
        obs_high,
        obs_low,
        weight_x,
        weight_y,
    )
    adjoint = solve_field(finish(partial))
    hess_vec = -basal_drag * (state_vel[0] * adjoint[0] + state_vel[1] * adjoint[1])
    return (tangent_vel, hess_vec)


def solution(mesh):
    placed = (
        P(None, ("groups", "wide"), "narrow"),
        P(("groups", "wide"), "narrow"),
        P(("groups", "wide"), "narrow"),
        P(("groups", "wide"), "narrow"),
        P(None, ("groups", "wide", "narrow", "sub")),
        P(None, ("groups", "wide", "narrow", "sub")),
        P(("groups", "wide", "narrow", "sub")),
        P(("groups", "wide", "narrow")),
        P(("groups", "wide", "narrow", "sub"), None),
        P(("groups", "wide", "narrow", "sub")),
        P(("groups", "wide", "narrow", "sub")),
        P(None, ("groups", "wide", "narrow", "sub")),
        P(None, ("groups", "wide", "narrow", "sub")),
        P(("groups", "wide", "narrow", "sub")),
    )
    return jax.shard_map(
        per_device,
        mesh=mesh,
        in_specs=placed,
        out_specs=(P(None, ("groups", "wide"), "narrow"), P(("groups", "wide"), "narrow")),
        check_vma=False,
    )
```

time: 1480 us -> 706 us (0.48)
  other arithmetic: 666 us -> 15.4 us
  local copies, waits for them, and re-layouts: 388 us -> 182 us
  Pallas kernels: 0 us -> 69.4 us
  blocking collectives: 112 us -> 131 us
    scatter-add x10, other arithmetic: 645 us -> 0.09 us  [reduce_rims(): middle.at[:, :, 0].add(beside[:, :, 0]).at[:, :, -1].add(beside[:, :, 3])]
    gather x17 -> x0, local copies, waits for them, and re-layouts: 313 us -> none  [the longest x8 199 us: operate(): values = spread(field)[:, vertex_ids]]
    scatter-add x10, local copies, waits for them, and re-layouts: 0.35 us -> 129 us  [reduce_rims(): return interior.at[:, 0].add(across[:, 0]).at[:, -1].add(across[:, 3])]
    pallas_call x0 -> x7, Pallas kernels: none -> 69.4 us  [call(): pl.pallas_call(kernel, out_shape=jax.ShapeDtypeStruct(out, jnp.float32),...]
    reshape x19 -> x0, local copies, waits for them, and re-layouts: 37 us -> none  [the longest x12 32.2 us: spread(): return ghosted(field).reshape(2, padded_count)]
    ppermute x22, waiting for transfers between devices: 3.6 us -> 21.1 us  [padded(): lax.ppermute(lax.slice_in_dim(block, block.shape[dim] - width, None, axis...]
    ppermute x22, waiting for transfers between devices: 69.8 us -> 53.3 us  [padded(): lax.ppermute(lax.slice_in_dim(block, 0, width, axis=dim), axis, backward)]
  transfers between devices with their start and end apart: 53 -> 50, of which waited for: 31 -> 31; matrix products, arithmetic and copies ran while one was open for 10% -> 5% of each run, Pallas kernels for 0% -> 0%
where the time goes in v1:
time: 706 us; the launch traced here: 697 us
  local copies, waits for them, and re-layouts  182 us (26%)
  waiting for transfers between devices  170 us (24%)
  blocking collectives  131 us (19%)
  starting transfers between devices  105 us (15%)
  Pallas kernels  69.4 us (10%)
  between operations  23.5 us (3%)
  other arithmetic  15.4 us (2%)
    scatter-add x10, local copies, waits for them, and re-layouts, reduce_rims(): return interior.at[:, 0].add(across[:, 0]).at[:, -1].add(across[:, 3])  129 us
    psum x5, waiting for transfers between devices, finish(): both = lax.psum(partial, 'sub')  89.4 us
    psum x4, blocking collectives, norm_sum(): return lax.psum(jnp.sum(residual * residual), ('wide', 'narrow'))  78.6 us
    ppermute x22, starting transfers between devices, padded(): lax.ppermute(lax.slice_in_dim(block, block.shape[dim] - width, None, axis...  72.9 us
    pallas_call x7, Pallas kernels, call(): pl.pallas_call(kernel, out_shape=jax.ShapeDtypeStruct(out, jnp.float32),...  69.4 us
    ppermute x22, waiting for transfers between devices, padded(): lax.ppermute(lax.slice_in_dim(block, 0, width, axis=dim), axis, backward)  53.3 us
    psum x2, blocking collectives, solve_field(): lax.psum(jnp.sum(direction * applied), ('wide', 'narrow'))  43.2 us
    ppermute x22, starting transfers between devices, padded(): lax.ppermute(lax.slice_in_dim(block, 0, width, axis=dim), axis, backward)  28.8 us
  transfers between devices with their start and end apart: 50, of which 31 were waited for; matrix products, arithmetic and copies ran while one was open for 5% of the time, Pallas kernels for 0%

profile of v1, /device:TPU:0, one launch (start us, length us, event | category | flops | bytes accessed | tf_op | source)
XLA Modules:
  0.0 696.5 jit_solution(4908753429375710669)
XLA Ops:
  10.6 4.9 collective-permute-start
  17.0 4.7 collective-permute-start.4
  31.1 4.5 collective-permute-start.6
  41.3 5.3 shard_map.149.coef_ref
  46.6 14.0 %shard_map.150 = f32[2,72,256]{2,1,0:T(8,128)S(1)} custom-call(f32[2,72,256]{2,1,0:T(8,128)S(1)} %copy.164.field_ref, s32[3,6144]{1,0:T(4,128)S(1)} %get-tuple-element.297.high_ref, s32[3,6144]{1,0:T(4,128)S(1)} %get-tuple-element.296.low_ref, f32[7,6144]{1,0:T(8,128)S(1)} %copy-done, f32[1,6144]{1,0:T(1,128)S(1)} %shard_map.149.coef_ref), custom_call_target="tpu_custom_call" | custom-call | tf_op jit(solution)/shard_map/pallas_call | solution.py:232
  61.6 20.4 %all-reduce.23.cloned.1.call-done = f32[2,72,256]{1,0,2:T(2,128)} async-done(((f32[2,72,256]{1,0,2:T(2,128)}), f32[2,72,256]{1,0,2:T(2,128)}) %all-reduce.23.cloned.1.call-update) | async-done | bytes 147472 | tf_op jit(solution)/shard_map/psum | solution.py:320
  105.9 21.5 %scatter-add.71 = f32[2,64,256]{1,0,2:T(2,128)S(1)} dynamic-update-slice(f32[2,64,256]{1,0,2:T(2,128)S(1)} %scatter-add.70, f32[2,1,256]{1,0,2:T(2,128)S(1)} %slice_add_fusion.8, s32[]{:T(128)} %constant.498.clone.1, s32[]{:T(128)} %constant.509.clone.1, s32[]{:T(128)} %constant.498.clone.1) | dynamic-update-slice | bytes 4100 | tf_op jit(solution)/shard_map/scatter-add | solution.py:277
  128.5 21.6 %all-reduce.16 = (f32[]{:T(128)}, f32[]{:T(128)}) all-reduce(f32[]{:T(128)} %get-tuple-element.253, f32[]{:T(128)} %get-tuple-element.252), channel_id=1, replica_groups=mesh['groups'=2,'wide'=4,'narrow'=2,'sub'=2] {'wide','narrow'}, use_global_device_ids=true, to_apply=%region_1.2 | all-reduce | flops 2 | bytes 16 | tf_op jit(solution)/shard_map/psum | solution.py:281
  152.5 17.8 %psum.94 = f32[]{:T(128)} all-reduce(f32[]{:T(128)} %multiply_reduce_fusion.5), channel_id=1, replica_groups=mesh['groups'=2,'wide'=4,'narrow'=2,'sub'=2] {'wide','narrow'}, use_global_device_ids=true, to_apply=%region_6.7 | all-reduce | flops 1 | bytes 8 | tf_op jit(solution)/shard_map/psum | solution.py:281
  177.3 4.4 collective-permute-done.13
  193.5 14.0 %shard_map.151 = f32[2,72,256]{2,1,0:T(8,128)S(1)} custom-call(f32[2,72,256]{2,1,0:T(8,128)S(1)} %copy.169.field_ref, s32[3,6144]{1,0:T(4,128)S(1)} %get-tuple-element.297.high_ref, s32[3,6144]{1,0:T(4,128)S(1)} %get-tuple-element.296.low_ref, f32[7,6144]{1,0:T(8,128)S(1)} %copy-done, f32[1,6144]{1,0:T(1,128)S(1)} %shard_map.149.coef_ref), custom_call_target="tpu_custom_call" | custom-call | tf_op jit(solution)/shard_map/pallas_call | solution.py:232
  208.5 16.7 %all-reduce.25.cloned.1.call-done = f32[2,72,256]{1,0,2:T(2,128)} async-done(((f32[2,72,256]{1,0,2:T(2,128)}), f32[2,72,256]{1,0,2:T(2,128)}) %all-reduce.25.cloned.1.call-update) | async-done | bytes 147472 | tf_op jit(solution)/shard_map/psum | solution.py:320
  249.1 21.5 %scatter-add.79 = f32[2,64,256]{1,0,2:T(2,128)S(1)} dynamic-update-slice(f32[2,64,256]{1,0,2:T(2,128)S(1)} %scatter-add.76, f32[2,1,256]{1,0,2:T(2,128)S(1)} %slice_add_fusion.6, s32[]{:T(128)} %constant.498.clone.1, s32[]{:T(128)} %constant.509.clone.1, s32[]{:T(128)} %constant.498.clone.1) | dynamic-update-slice | bytes 4100 | tf_op jit(solution)/shard_map/scatter-add | solution.py:277
  271.5 21.6 %psum.96 = f32[]{:T(128)} all-reduce(f32[]{:T(128)} %multiply_reduce_fusion.4), channel_id=1, replica_groups=mesh['groups'=2,'wide'=4,'narrow'=2,'sub'=2] {'wide','narrow'}, use_global_device_ids=true, to_apply=%region_9.10 | all-reduce | flops 1 | bytes 8 | tf_op jit(solution)/shard_map/psum | solution.py:350
  300.1 4.4 collective-permute-done.21
  321.1 6.5 all-to-all-done
  327.6 11.8 %gather_fusion = f32[2048]{0:T(1024)S(1)} fusion(f32[4096]{0:T(1024)S(1)} %bitcast.98, s32[2048]{0:T(1024)S(1)} %broadcast_clamp_fusion), kind=kCustom, calls=%fused_computation | custom fusion | bytes 24576 | tf_op jit(solution)/shard_map/gather | solution.py:380
  339.5 8.1 %scatter_custom_fusion = f32[4096]{0:T(1024)S(1)} fusion(s32[2048]{0:T(1024)S(1)} %bitcast.118, f32[2048]{0:T(1024)S(1)} %subtract_bitcast_fusion, f32[]{:T(128)} %constant.496.clone.1), kind=kCustom, calls=%fused_computation.78 | custom fusion | bytes 16388 | tf_op jit(solution)/shard_map/scatter | solution.py:384
  347.6 8.9 %all_to_all.18 = f32[8,1,512]{2,1,0:T(1,128)S(1)} all-to-all(f32[8,1,512]{2,1,0:T(1,128)S(1)} %bitcast.116), channel_id=1, replica_groups=mesh['groups'=2,'wide'=4,'narrow'=2,'sub'=2] {'wide','narrow'}, dimensions={0} | all-to-all | bytes 32768 | tf_op jit(solution)/shard_map/all_to_all | solution.py:387
  361.5 15.7 %all-reduce.27.cloned.1.call-done = f32[2,72,256]{1,0,2:T(2,128)} async-done(((f32[2,72,256]{1,0,2:T(2,128)}), f32[2,72,256]{1,0,2:T(2,128)}) %all-reduce.27.cloned.1.call-update) | async-done | bytes 147472 | tf_op jit(solution)/shard_map/psum | solution.py:320
  401.0 21.5 %scatter-add.85 = f32[2,64,256]{1,0,2:T(2,128)S(1)} dynamic-update-slice(f32[2,64,256]{1,0,2:T(2,128)S(1)} %scatter-add.84, f32[2,1,256]{1,0,2:T(2,128)S(1)} %slice_add_fusion.4, s32[]{:T(128)} %constant.498.clone.1, s32[]{:T(128)} %constant.509.clone.1, s32[]{:T(128)} %constant.498.clone.1) | dynamic-update-slice | bytes 4100 | tf_op jit(solution)/shard_map/scatter-add | solution.py:277
  423.8 5.0 collective-permute-start.28
  442.5 14.0 %shard_map.154 = f32[2,72,256]{2,1,0:T(8,128)S(1)} custom-call(f32[2,72,256]{2,1,0:T(8,128)S(1)} %copy.180.field_ref, s32[3,6144]{1,0:T(4,128)S(1)} %get-tuple-element.297.high_ref, s32[3,6144]{1,0:T(4,128)S(1)} %get-tuple-element.296.low_ref, f32[7,6144]{1,0:T(8,128)S(1)} %copy-done, f32[1,6144]{1,0:T(1,128)S(1)} %shard_map.149.coef_ref), custom_call_target="tpu_custom_call" | custom-call | tf_op jit(solution)/shard_map/pallas_call | solution.py:232
  457.4 19.8 %all-reduce.29.cloned.1.call-done = f32[2,72,256]{1,0,2:T(2,128)} async-done(((f32[2,72,256]{1,0,2:T(2,128)}), f32[2,72,256]{1,0,2:T(2,128)}) %all-reduce.29.cloned.1.call-update) | async-done | bytes 147472 | tf_op jit(solution)/shard_map/psum | solution.py:320
  501.1 21.5 %scatter-add.91 = f32[2,64,256]{1,0,2:T(2,128)S(1)} dynamic-update-slice(f32[2,64,256]{1,0,2:T(2,128)S(1)} %scatter-add.90, f32[2,1,256]{1,0,2:T(2,128)S(1)} %slice_add_fusion.2, s32[]{:T(128)} %constant.498.clone.1, s32[]{:T(128)} %constant.509.clone.1, s32[]{:T(128)} %constant.498.clone.1) | dynamic-update-slice | bytes 4100 | tf_op jit(solution)/shard_map/scatter-add | solution.py:277
  523.7 21.6 %all-reduce.15 = (f32[]{:T(128)}, f32[]{:T(128)}) all-reduce(f32[]{:T(128)} %get-tuple-element.251, f32[]{:T(128)} %get-tuple-element.250), channel_id=1, replica_groups=mesh['groups'=2,'wide'=4,'narrow'=2,'sub'=2] {'wide','narrow'}, use_global_device_ids=true, to_apply=%region_16.17 | all-reduce | flops 2 | bytes 16 | tf_op jit(solution)/shard_map/psum | solution.py:281
  547.4 17.7 %psum.101 = f32[]{:T(128)} all-reduce(f32[]{:T(128)} %multiply_reduce_fusion.1), channel_id=1, replica_groups=mesh['groups'=2,'wide'=4,'narrow'=2,'sub'=2] {'wide','narrow'}, use_global_device_ids=true, to_apply=%region_21.22 | all-reduce | flops 1 | bytes 8 | tf_op jit(solution)/shard_map/psum | solution.py:281
  572.3 4.4 collective-permute-done.37
  586.4 14.0 %shard_map.155 = f32[2,72,256]{2,1,0:T(8,128)S(1)} custom-call(f32[2,72,256]{2,1,0:T(8,128)S(1)} %concatenate.133.field_ref, s32[3,6144]{1,0:T(4,128)S(1)} %get-tuple-element.297.high_ref, s32[3,6144]{1,0:T(4,128)S(1)} %get-tuple-element.296.low_ref, f32[7,6144]{1,0:T(8,128)S(1)} %copy-done, f32[1,6144]{1,0:T(1,128)S(1)} %shard_map.149.coef_ref), custom_call_target="tpu_custom_call" | custom-call | tf_op jit(solution)/shard_map/pallas_call | solution.py:232
  601.3 16.8 %all-reduce.31.cloned.1.call-done = f32[2,72,256]{1,0,2:T(2,128)} async-done(((f32[2,72,256]{1,0,2:T(2,128)}), f32[2,72,256]{1,0,2:T(2,128)}) %all-reduce.31.cloned.1.call-update) | async-done | bytes 147472 | tf_op jit(solution)/shard_map/psum | solution.py:320
  641.9 21.5 %scatter-add.99 = f32[2,64,256]{1,0,2:T(2,128)S(1)} dynamic-update-slice(f32[2,64,256]{1,0,2:T(2,128)S(1)} %scatter-add.96, f32[2,1,256]{1,0,2:T(2,128)S(1)} %slice_add_fusion, s32[]{:T(128)} %constant.498.clone.1, s32[]{:T(128)} %constant.509.clone.1, s32[]{:T(128)} %constant.498.clone.1) | dynamic-update-slice | bytes 4100 | tf_op jit(solution)/shard_map/scatter-add | solution.py:277
  665.1 21.6 %psum.103 = f32[]{:T(128)} all-reduce(f32[]{:T(128)} %multiply_reduce_fusion), channel_id=1, replica_groups=mesh['groups'=2,'wide'=4,'narrow'=2,'sub'=2] {'wide','narrow'}, use_global_device_ids=true, to_apply=%region_24.25 | all-reduce | flops 1 | bytes 8 | tf_op jit(solution)/shard_map/psum | solution.py:350
  (277 shorter events, 225.5 us)
Async XLA Ops:
  7.2 74.8 %all-reduce.23.cloned.1.call-start = ((), (), s32[]{:S(2)}) async-start(), calls=%async_computation.2 | async-start | bytes 524288 | tf_op jit(solution)/shard_map/psum | solution.py:320
  10.6 15.6 %collective-permute-start = (f32[2,1,256]{1,0,2:T(2,128)S(1)}, f32[2,1,256]{1,0,2:T(2,128)S(1)}, u32[]{:S(2)}, u32[]{:S(2)}) collective-permute-start(f32[2,1,256]{1,0,2:T(2,128)S(1)} %get-tuple-element.291), channel_id=1, source_target_pairs={{0,4},{4,8},{8,12},{1,5},{5,9},{9,13},{2,6},{6,10},{10,14},{3,7},{... | collective-permute-start | bytes 6152 | tf_op jit(solution)/shard_map/ppermute | solution.py:23
  15.5 10.6 %collective-permute-start.1 = (f32[2,1,256]{1,0,2:T(2,128)S(1)}, f32[2,1,256]{1,0,2:T(2,128)S(1)}, u32[]{:S(2)}, u32[]{:S(2)}) collective-permute-start(f32[2,1,256]{1,0,2:T(2,128)S(1)} %get-tuple-element.290), channel_id=1, source_target_pairs={{4,0},{8,4},{12,8},{5,1},{9,5},{13,9},{6,2},{10,6},{14,10},{7,3},{... | collective-permute-start | bytes 6152 | tf_op jit(solution)/shard_map/ppermute | solution.py:26
  17.0 13.9 %collective-permute-start.4 = (f32[2,1,256]{1,0,2:T(2,128)S(1)}, f32[2,1,256]{1,0,2:T(2,128)S(1)}, u32[]{:S(2)}, u32[]{:S(2)}) collective-permute-start(f32[2,1,256]{1,0,2:T(2,128)S(1)} %copy.159), channel_id=1, source_target_pairs={{0,4},{4,8},{8,12},{1,5},{5,9},{9,13},{2,6},{6,10},{10,14},{3,7},{... | collective-permute-start | bytes 6152 | tf_op jit(solution)/shard_map/ppermute | solution.py:23
  21.9 9.1 %collective-permute-start.5 = (f32[2,1,256]{1,0,2:T(2,128)S(1)}, f32[2,1,256]{1,0,2:T(2,128)S(1)}, u32[]{:S(2)}, u32[]{:S(2)}) collective-permute-start(f32[2,1,256]{1,0,2:T(2,128)S(1)} %copy.160), channel_id=1, source_target_pairs={{4,0},{8,4},{12,8},{5,1},{9,5},{13,9},{6,2},{10,6},{14,10},{7,3},{... | collective-permute-start | bytes 6152 | tf_op jit(solution)/shard_map/ppermute | solution.py:26
  26.3 10.9 %collective-permute-start.2 = (f32[2,66,1]{1,0,2:T(2,128)S(1)}, f32[2,66,1]{1,0,2:T(2,128)S(1)}, u32[]{:S(2)}, u32[]{:S(2)}) collective-permute-start(f32[2,66,1]{1,0,2:T(2,128)S(1)} %get-tuple-element.270), channel_id=1, source_target_pairs={{0,2},{1,3},{4,6},{5,7},{8,10},{9,11},{12,14},{13,15},{16,18},{17,... | collective-permute-start | bytes 1592 | tf_op jit(solution)/shard_map/ppermute | solution.py:23
  29.7 7.5 %collective-permute-start.3 = (f32[2,66,1]{1,0,2:T(2,128)S(1)}, f32[2,66,1]{1,0,2:T(2,128)S(1)}, u32[]{:S(2)}, u32[]{:S(2)}) collective-permute-start(f32[2,66,1]{1,0,2:T(2,128)S(1)} %get-tuple-element.271), channel_id=1, source_target_pairs={{2,0},{3,1},{6,4},{7,5},{10,8},{11,9},{14,12},{15,13},{18,16},{19,... | collective-permute-start | bytes 1592 | tf_op jit(solution)/shard_map/ppermute | solution.py:26
  31.1 8.5 %collective-permute-start.6 = (f32[2,66,1]{1,0,2:T(2,128)S(1)}, f32[2,66,1]{1,0,2:T(2,128)S(1)}, u32[]{:S(2)}, u32[]{:S(2)}) collective-permute-start(f32[2,66,1]{1,0,2:T(2,128)S(1)} %get-tuple-element.268), channel_id=1, source_target_pairs={{0,2},{1,3},{4,6},{5,7},{8,10},{9,11},{12,14},{13,15},{16,18},{17,... | collective-permute-start | bytes 1592 | tf_op jit(solution)/shard_map/ppermute | solution.py:23
  35.6 5.5 collective-permute-start.7
  61.5 163.7 %all-reduce.25.cloned.1.call-start = ((), (), s32[]{:S(2)}) async-start(), calls=%async_computation.3 | async-start | bytes 524288 | tf_op jit(solution)/shard_map/psum | solution.py:320
  87.1 5.5 collective-permute-start.9
  93.0 8.0 %collective-permute-start.10 = (f32[2,1,256]{1,0,2:T(2,128)S(1)}, f32[2,1,256]{1,0,2:T(2,128)S(1)}, u32[]{:S(2)}, u32[]{:S(2)}) collective-permute-start(f32[2,1,256]{1,0,2:T(2,128)S(1)} %get-tuple-element.289), channel_id=1, source_target_pairs={{0,4},{4,8},{8,12},{1,5},{5,9},{9,13},{2,6},{6,10},{10,14},{3,7},{... | collective-permute-start | bytes 6152 | tf_op jit(solution)/shard_map/ppermute | solution.py:23
  96.8 8.8 %collective-permute-start.11 = (f32[2,1,256]{1,0,2:T(2,128)S(1)}, f32[2,1,256]{1,0,2:T(2,128)S(1)}, u32[]{:S(2)}, u32[]{:S(2)}) collective-permute-start(f32[2,1,256]{1,0,2:T(2,128)S(1)} %get-tuple-element.288), channel_id=1, source_target_pairs={{4,0},{8,4},{12,8},{5,1},{9,5},{13,9},{6,2},{10,6},{14,10},{7,3},{... | collective-permute-start | bytes 6152 | tf_op jit(solution)/shard_map/ppermute | solution.py:26
  173.5 8.3 %collective-permute-start.13 = (f32[2,1,256]{1,0,2:T(2,128)S(1)}, f32[2,1,256]{1,0,2:T(2,128)S(1)}, u32[]{:S(2)}, u32[]{:S(2)}) collective-permute-start(f32[2,1,256]{1,0,2:T(2,128)S(1)} %get-tuple-element.286), channel_id=1, source_target_pairs={{4,0},{8,4},{12,8},{5,1},{9,5},{13,9},{6,2},{10,6},{14,10},{7,3},{... | collective-permute-start | bytes 6152 | tf_op jit(solution)/shard_map/ppermute | solution.py:26
  181.8 5.8 collective-permute-start.14
  236.2 8.0 %collective-permute-start.18 = (f32[2,1,256]{1,0,2:T(2,128)S(1)}, f32[2,1,256]{1,0,2:T(2,128)S(1)}, u32[]{:S(2)}, u32[]{:S(2)}) collective-permute-start(f32[2,1,256]{1,0,2:T(2,128)S(1)} %get-tuple-element.285), channel_id=1, source_target_pairs={{0,4},{4,8},{8,12},{1,5},{5,9},{9,13},{2,6},{6,10},{10,14},{3,7},{... | collective-permute-start | bytes 6152 | tf_op jit(solution)/shard_map/ppermute | solution.py:23
  239.9 8.8 %collective-permute-start.19 = (f32[2,1,256]{1,0,2:T(2,128)S(1)}, f32[2,1,256]{1,0,2:T(2,128)S(1)}, u32[]{:S(2)}, u32[]{:S(2)}) collective-permute-start(f32[2,1,256]{1,0,2:T(2,128)S(1)} %get-tuple-element.284), channel_id=1, source_target_pairs={{4,0},{8,4},{12,8},{5,1},{9,5},{13,9},{6,2},{10,6},{14,10},{7,3},{... | collective-permute-start | bytes 6152 | tf_op jit(solution)/shard_map/ppermute | solution.py:26
  296.2 8.3 %collective-permute-start.21 = (f32[2,1,256]{1,0,2:T(2,128)S(1)}, f32[2,1,256]{1,0,2:T(2,128)S(1)}, u32[]{:S(2)}, u32[]{:S(2)}) collective-permute-start(f32[2,1,256]{1,0,2:T(2,128)S(1)} %get-tuple-element.282), channel_id=1, source_target_pairs={{4,0},{8,4},{12,8},{5,1},{9,5},{13,9},{6,2},{10,6},{14,10},{7,3},{... | collective-permute-start | bytes 6152 | tf_op jit(solution)/shard_map/ppermute | solution.py:26
  317.6 9.9 %all-to-all-start = ((f32[8,1,512]{2,1,0:T(1,128)}), f32[8,1,512]{2,1,0:T(1,128)S(1)}, u32[]{:S(2)}, u32[]{:S(2)}) async-start(f32[8,1,512]{2,1,0:T(1,128)} %bitcast.26), calls=%async_computation | async-start | bytes 32768 | tf_op jit(solution)/shard_map/all_to_all | solution.py:374
  321.0 56.1 %all-reduce.27.cloned.1.call-start = ((), (), s32[]{:S(2)}) async-start(), calls=%async_computation.4 | async-start | bytes 524288 | tf_op jit(solution)/shard_map/psum | solution.py:320
  361.4 115.9 %all-reduce.29.cloned.1.call-start = ((), (), s32[]{:S(2)}) async-start(), calls=%async_computation.5 | async-start | bytes 524288 | tf_op jit(solution)/shard_map/psum | solution.py:320
  388.0 8.0 %collective-permute-start.26 = (f32[2,1,256]{1,0,2:T(2,128)S(1)}, f32[2,1,256]{1,0,2:T(2,128)S(1)}, u32[]{:S(2)}, u32[]{:S(2)}) collective-permute-start(f32[2,1,256]{1,0,2:T(2,128)S(1)} %get-tuple-element.281), channel_id=1, source_target_pairs={{0,4},{4,8},{8,12},{1,5},{5,9},{9,13},{2,6},{6,10},{10,14},{3,7},{... | collective-permute-start | bytes 6152 | tf_op jit(solution)/shard_map/ppermute | solution.py:23
  392.0 8.7 %collective-permute-start.27 = (f32[2,1,256]{1,0,2:T(2,128)S(1)}, f32[2,1,256]{1,0,2:T(2,128)S(1)}, u32[]{:S(2)}, u32[]{:S(2)}) collective-permute-start(f32[2,1,256]{1,0,2:T(2,128)S(1)} %get-tuple-element.280), channel_id=1, source_target_pairs={{4,0},{8,4},{12,8},{5,1},{9,5},{13,9},{6,2},{10,6},{14,10},{7,3},{... | collective-permute-start | bytes 6152 | tf_op jit(solution)/shard_map/ppermute | solution.py:26
  422.5 8.7 %collective-permute-start.29 = (f32[2,1,256]{1,0,2:T(2,128)S(1)}, f32[2,1,256]{1,0,2:T(2,128)S(1)}, u32[]{:S(2)}, u32[]{:S(2)}) collective-permute-start(f32[2,1,256]{1,0,2:T(2,128)S(1)} %bitcast.99), channel_id=1, source_target_pairs={{4,0},{8,4},{12,8},{5,1},{9,5},{13,9},{6,2},{10,6},{14,10},{7,3},{... | collective-permute-start | bytes 6152 | tf_op jit(solution)/shard_map/ppermute | solution.py:26
  423.8 8.8 %collective-permute-start.28 = (f32[2,1,256]{1,0,2:T(2,128)S(1)}, f32[2,1,256]{1,0,2:T(2,128)S(1)}, u32[]{:S(2)}, u32[]{:S(2)}) collective-permute-start(f32[2,1,256]{1,0,2:T(2,128)S(1)} %slice_add_fusion.4), channel_id=1, source_target_pairs={{0,4},{4,8},{8,12},{1,5},{5,9},{9,13},{2,6},{6,10},{10,14},{3,7},{... | collective-permute-start | bytes 6152 | tf_op jit(solution)/shard_map/ppermute | solution.py:23
  457.4 160.7 %all-reduce.31.cloned.1.call-start = ((), (), s32[]{:S(2)}) async-start(), calls=%async_computation.6 | async-start | bytes 524288 | tf_op jit(solution)/shard_map/psum | solution.py:320
  488.2 8.0 %collective-permute-start.34 = (f32[2,1,256]{1,0,2:T(2,128)S(1)}, f32[2,1,256]{1,0,2:T(2,128)S(1)}, u32[]{:S(2)}, u32[]{:S(2)}) collective-permute-start(f32[2,1,256]{1,0,2:T(2,128)S(1)} %get-tuple-element.279), channel_id=1, source_target_pairs={{0,4},{4,8},{8,12},{1,5},{5,9},{9,13},{2,6},{6,10},{10,14},{3,7},{... | collective-permute-start | bytes 6152 | tf_op jit(solution)/shard_map/ppermute | solution.py:23
  491.9 8.8 %collective-permute-start.35 = (f32[2,1,256]{1,0,2:T(2,128)S(1)}, f32[2,1,256]{1,0,2:T(2,128)S(1)}, u32[]{:S(2)}, u32[]{:S(2)}) collective-permute-start(f32[2,1,256]{1,0,2:T(2,128)S(1)} %get-tuple-element.278), channel_id=1, source_target_pairs={{4,0},{8,4},{12,8},{5,1},{9,5},{13,9},{6,2},{10,6},{14,10},{7,3},{... | collective-permute-start | bytes 6152 | tf_op jit(solution)/shard_map/ppermute | solution.py:26
  568.4 8.3 %collective-permute-start.37 = (f32[2,1,256]{1,0,2:T(2,128)S(1)}, f32[2,1,256]{1,0,2:T(2,128)S(1)}, u32[]{:S(2)}, u32[]{:S(2)}) collective-permute-start(f32[2,1,256]{1,0,2:T(2,128)S(1)} %get-tuple-element.276), channel_id=1, source_target_pairs={{4,0},{8,4},{12,8},{5,1},{9,5},{13,9},{6,2},{10,6},{14,10},{7,3},{... | collective-permute-start | bytes 6152 | tf_op jit(solution)/shard_map/ppermute | solution.py:26
  576.7 5.9 collective-permute-start.38
  629.0 8.0 %collective-permute-start.42 = (f32[2,1,256]{1,0,2:T(2,128)S(1)}, f32[2,1,256]{1,0,2:T(2,128)S(1)}, u32[]{:S(2)}, u32[]{:S(2)}) collective-permute-start(f32[2,1,256]{1,0,2:T(2,128)S(1)} %get-tuple-element.275), channel_id=1, source_target_pairs={{0,4},{4,8},{8,12},{1,5},{5,9},{9,13},{2,6},{6,10},{10,14},{3,7},{... | collective-permute-start | bytes 6152 | tf_op jit(solution)/shard_map/ppermute | solution.py:23
  632.7 8.8 %collective-permute-start.43 = (f32[2,1,256]{1,0,2:T(2,128)S(1)}, f32[2,1,256]{1,0,2:T(2,128)S(1)}, u32[]{:S(2)}, u32[]{:S(2)}) collective-permute-start(f32[2,1,256]{1,0,2:T(2,128)S(1)} %get-tuple-element.274), channel_id=1, source_target_pairs={{4,0},{8,4},{12,8},{5,1},{9,5},{13,9},{6,2},{10,6},{14,10},{7,3},{... | collective-permute-start | bytes 6152 | tf_op jit(solution)/shard_map/ppermute | solution.py:26
  (35 other events, 138.8 us)
Sparse Core Ops, SparseCore 0:
  61.7 20.2 all-reduce.22
  208.5 16.6 all-reduce.24
  361.5 15.5 all-reduce.26
  457.5 19.7 all-reduce.28
  601.4 16.6 all-reduce.30

commit v2 on v1

--- a/solution.py
+++ b/solution.py
@@ -400,6 +400,550 @@
     return (tangent_vel, hess_vec)
 
 
+def node_ids(ids, node_rows, columns):
+    row = ids // (columns + 2)
+    col = ids % (columns + 2)
+    left, right = col == 0, col == columns + 1
+    inner = jnp.where(row == 0, node_rows, jnp.where(row == node_rows + 1, row, row - 1))
+    high = jnp.where(left | right, node_rows + 2, inner)
+    low = jnp.where(left, row, jnp.where(right, row + RIM, col - 1))
+    return high, low
+
+
+SIDES = [(dw, dn) for dw in (-1, 0, 1) for dn in (-1, 0, 1)]
+TILE = 8
+
+
+def whole_kernel(
+    wide,
+    narrow,
+    state_ref,
+    friction_ref,
+    area_ref,
+    beta_ref,
+    high_ref,
+    low_ref,
+    geom_ref,
+    scale_ref,
+    dest_ref,
+    prec_ref,
+    couple_ref,
+    obs_high_ref,
+    obs_low_ref,
+    wx_ref,
+    wy_ref,
+    tangent_ref,
+    hess_ref,
+    stack_ref,
+    total_ref,
+    coef_ref,
+    drag_ref,
+    vel_ref,
+    p_ref,
+    r_ref,
+    x_ref,
+    q_ref,
+    field_send,
+    field_recv,
+    rim_send,
+    rim_recv,
+    sum_send,
+    sum_recv,
+    pix_send,
+    pix_recv,
+    field_ss,
+    field_rs,
+    rim_ss,
+    rim_rs,
+    sum_ss,
+    sum_rs,
+    pix_ss,
+    pix_rs,
+):
+    node_rows, columns = friction_ref.shape
+    rows = vel_ref.shape[1]
+    count = wide * narrow
+    my_w = lax.axis_index("wide")
+    my_n = lax.axis_index("narrow")
+    my_s = lax.axis_index("sub")
+    me = my_w * narrow + my_n
+    f32 = jnp.float32
+
+    def place_of(q):
+        return {"wide": q // narrow, "narrow": lax.rem(q, narrow), "sub": my_s}
+
+    partner = {"wide": my_w, "narrow": my_n, "sub": 1 - my_s}
+    barrier = pltpu.get_barrier_semaphore()
+    pl.semaphore_signal(barrier, inc=1, device_id=partner, device_id_type=pl.DeviceIdType.MESH)
+    for k in range(1, count):
+        pl.semaphore_signal(
+            barrier,
+            inc=1,
+            device_id=place_of(lax.rem(me + k, count)),
+            device_id_type=pl.DeviceIdType.MESH,
+        )
+    pl.semaphore_wait(barrier, count)
+
+    row_at = lax.broadcasted_iota(jnp.int32, (rows, columns), 0)
+    lane_at = lax.broadcasted_iota(jnp.int32, (rows, columns), 1)
+    eye_row = lax.broadcasted_iota(jnp.int32, (rows, RIM), 0)
+    eye_lane = lax.broadcasted_iota(jnp.int32, (rows, RIM), 1)
+    eye_row = jnp.where(
+        eye_row < node_rows,
+        eye_row + 1,
+        jnp.where(eye_row == node_rows, 0, jnp.where(eye_row == node_rows + 1, eye_row, -1)),
+    )
+    eye = eye_row == eye_lane
+    rim_lane = lax.broadcasted_iota(jnp.int32, (1, RIM), 1)
+
+    def exists(dw, dn):
+        w, n = my_w + dw, my_n + dn
+        return (w >= 0) & (w < wide) & (n >= 0) & (n < narrow)
+
+    has_up, has_down = my_w > 0, my_w < wide - 1
+    has_left, has_right = my_n > 0, my_n < narrow - 1
+    rim_row = jnp.where(lane_at >= RIM, lane_at - RIM, lane_at)
+    rim_side = ((lane_at < RIM) & has_left) | ((lane_at >= RIM) & has_right)
+    rim_in = (
+        ((rim_row >= 1) & (rim_row <= node_rows))
+        | ((rim_row == 0) & has_up)
+        | ((rim_row == node_rows + 1) & has_down)
+    )
+    inside = (
+        (row_at < node_rows)
+        | ((row_at == node_rows) & has_up)
+        | ((row_at == node_rows + 1) & has_down)
+        | ((row_at == node_rows + 2) & rim_side & rim_in)
+    )
+
+    def col_lanes(field, lane):
+        column = field[:, lane : lane + 1]
+        return jnp.sum(jnp.where(eye, column, 0.0), axis=0, keepdims=True)
+
+    def lanes_col(lanes):
+        return jnp.sum(jnp.where(eye, lanes, 0.0), axis=1, keepdims=True)
+
+    def rim_copy(k, slot):
+        dw, dn = SIDES[slot]
+        return pltpu.make_async_remote_copy(
+            src_ref=rim_send.at[k],
+            dst_ref=rim_recv.at[k, 8 - slot],
+            send_sem=rim_ss.at[k, slot],
+            recv_sem=rim_rs.at[k, 8 - slot],
+            device_id={"wide": my_w + dw, "narrow": my_n + dn, "sub": my_s},
+            device_id_type=pl.DeviceIdType.MESH,
+        )
+
+    def rim_landed(k, slot):
+        dw, dn = SIDES[slot]
+        return pltpu.make_async_remote_copy(
+            src_ref=rim_send.at[k],
+            dst_ref=rim_recv.at[k, slot],
+            send_sem=rim_ss.at[k, slot],
+            recv_sem=rim_rs.at[k, slot],
+            device_id={"wide": my_w + dw, "narrow": my_n + dn, "sub": my_s},
+            device_id_type=pl.DeviceIdType.MESH,
+        )
+
+    def rim_start(k, fields):
+        lines = []
+        for at in (node_rows, 0, node_rows - 1, node_rows + 1, node_rows + 2):
+            lines += [field[at : at + 1] for field in fields]
+        lines += [
+            jnp.concatenate([col_lanes(field, 0), col_lanes(field, columns - 1)], axis=1)
+            for field in fields
+        ]
+        for i, line in enumerate(lines):
+            rim_send[k, i : i + 1, :] = line
+        for slot, side in enumerate(SIDES):
+            if side != (0, 0):
+
+                @pl.when(exists(*side))
+                def _():
+                    rim_copy(k, slot).start()
+
+    def moved(lanes, dw):
+        if dw == 0:
+            return lanes
+        if dw < 0:
+            turned = pltpu.roll(lanes, (RIM - node_rows) % RIM, 1)
+            return jnp.where(rim_lane < 2, turned, 0.0)
+        turned = pltpu.roll(lanes, node_rows, 1)
+        keep = (rim_lane == node_rows) | (rim_lane == node_rows + 1)
+        return jnp.where(keep, turned, 0.0)
+
+    def rim_finish(k, fields):
+        for slot, side in enumerate(SIDES):
+            if side != (0, 0):
+
+                @pl.when(exists(*side))
+                def _():
+                    rim_landed(k, slot).wait_recv()
+                    rim_landed(k, slot).wait_send()
+
+        done = []
+        for c, field in enumerate(fields):
+
+            def got(dw, dn, line, low, size):
+                slot = SIDES.index((dw, dn))
+                at = 2 * line + c
+                value = rim_recv[k, slot, at : at + 1, low : low + size]
+                return jnp.where(exists(dw, dn), value, 0.0)
+
+            left_rim = jnp.zeros((1, RIM), f32)
+            right_rim = jnp.zeros((1, RIM), f32)
+            left_col = jnp.zeros((1, RIM), f32)
+            right_col = jnp.zeros((1, RIM), f32)
+            for dw in (-1, 1):
+                left_rim = left_rim + moved(got(dw, 0, 4, 0, RIM), dw)
+                right_rim = right_rim + moved(got(dw, 0, 4, RIM, RIM), dw)
+            for dw in (0, -1, 1):
+                left_col = left_col + moved(got(dw, -1, 4, RIM, RIM), dw)
+                left_rim = left_rim + moved(got(dw, -1, 5, RIM, RIM), dw)
+                right_col = right_col + moved(got(dw, 1, 4, 0, RIM), dw)
+                right_rim = right_rim + moved(got(dw, 1, 5, 0, RIM), dw)
+            result = field
+            for at, dw, line in (
+                (node_rows, -1, 2),
+                (0, -1, 3),
+                (node_rows - 1, 1, 0),
+                (node_rows + 1, 1, 1),
+            ):
+                result = result + jnp.where(row_at == at, got(dw, 0, line, 0, columns), 0.0)
+            rim = jnp.concatenate([left_rim, right_rim], axis=1)
+            result = result + jnp.where(row_at == node_rows + 2, rim, 0.0)
+            result = result + jnp.where(lane_at == 0, lanes_col(left_col), 0.0)
+            result = result + jnp.where(lane_at == columns - 1, lanes_col(right_col), 0.0)
+            done.append(jnp.where(inside, result, 0.0))
+        return done
+
+    def all_copy(send, recv, ss, rs, k, target, slot):
+        return pltpu.make_async_remote_copy(
+            src_ref=send,
+            dst_ref=recv.at[k, slot],
+            send_sem=ss.at[k, target],
+            recv_sem=rs.at[k, slot],
+            device_id=place_of(target),
+            device_id_type=pl.DeviceIdType.MESH,
+        )
+
+    def sum_start(k, *values):
+        for i, value in enumerate(values):
+            sum_send[k, i : i + 1, :] = jnp.broadcast_to(value, (1, 128))
+        for j in range(1, count):
+            q = lax.rem(me + j, count)
+            all_copy(sum_send.at[k], sum_recv, sum_ss, sum_rs, k, q, me).start()
+        sum_recv[k, me] = sum_send[k]
+
+    def sum_finish(k):
+        for j in range(1, count):
+            q = lax.rem(me + j, count)
+            copy = all_copy(sum_send.at[k], sum_recv, sum_ss, sum_rs, k, q, q)
+            copy.wait_recv()
+            copy.wait_send()
+        total = sum_recv[k, 0]
+        for q in range(1, count):
+            total = total + sum_recv[k, q]
+        return total[0:1, 0:1], total[1:2, 0:1]
+
+    def pix_trade(k):
+        for j in range(1, count):
+            q = lax.rem(me + j, count)
+            all_copy(pix_send.at[k, q], pix_recv, pix_ss, pix_rs, k, q, me).start()
+        pix_recv[k, me] = pix_send[k, me]
+        for j in range(1, count):
+            q = lax.rem(me + j, count)
+            copy = all_copy(pix_send.at[k, q], pix_recv, pix_ss, pix_rs, k, q, q)
+            copy.wait_recv()
+            copy.wait_send()
+
+    def core_sum(k):
+        field_send[k, 0], field_send[k, 1] = unstack(total_ref[...])
+        copy = pltpu.make_async_remote_copy(
+            src_ref=field_send.at[k],
+            dst_ref=field_recv.at[k],
+            send_sem=field_ss.at[k],
+            recv_sem=field_rs.at[k],
+            device_id=partner,
+            device_id_type=pl.DeviceIdType.MESH,
+        )
+        copy.start()
+        copy.wait()
+        return [field_send[k, c] + field_recv[k, c] for c in range(2)]
+
+    def dot(a, b):
+        down = jnp.sum(a * b, axis=0, keepdims=True)
+        return jnp.sum(down, axis=1, keepdims=True)
+
+    def both(a_ref, b_ref, size):
+        return dot(a_ref[0, :size], b_ref[0, :size]) + dot(a_ref[1, :size], b_ref[1, :size])
+
+    def solve(field_at, rim_at, sum_at):
+        for c in range(2):
+            p_ref[c] = r_ref[c]
+        norm_now = None
+        for step in range(CG_ITERS):
+            stack_ref[...] = stack_field(p_ref)
+            operate_loop(stack_ref, high_ref, low_ref, geom_ref, coef_ref, total_ref, rows)
+            local = core_sum(field_at + step)
+            rim_start(rim_at + step, local)
+            energy = dot(local[0], p_ref[0]) + dot(local[1], p_ref[1])
+            for c in range(2):
+                field = p_ref[c, :node_rows]
+                energy = energy + dot(drag_ref[:node_rows] * field, field)
+            norm = both(r_ref, r_ref, node_rows)
+            sum_start(sum_at + 2 * step, norm, energy)
+            applied = rim_finish(rim_at + step, local)
+            for c in range(2):
+                q_ref[c] = applied[c] + drag_ref[...] * p_ref[c]
+            norm_now, energy = sum_finish(sum_at + 2 * step)
+            alpha = norm_now / energy
+            for c in range(2):
+                if step == 0:
+                    x_ref[c] = alpha * p_ref[c]
+                else:
+                    x_ref[c] = x_ref[c] + alpha * p_ref[c]
+            if step + 1 < CG_ITERS:
+                for c in range(2):
+                    r_ref[c] = r_ref[c] - alpha * q_ref[c]
+                norm = both(r_ref, r_ref, node_rows)
+                sum_start(sum_at + 2 * step + 1, norm)
+                norm_next, _ = sum_finish(sum_at + 2 * step + 1)
+                ratio = norm_next / norm_now
+                for c in range(2):
+                    p_ref[c] = r_ref[c] + ratio * p_ref[c]
+
+    sum_send[...] = jnp.zeros_like(sum_send)
+    rim_send[...] = jnp.zeros_like(rim_send)
+    pix_send[...] = jnp.zeros_like(pix_send)
+    gap = jnp.zeros((rows - node_rows, columns), f32)
+
+    def grown(value):
+        return jnp.concatenate([value, gap], axis=0)
+
+    vel = [grown(state_ref[0]), grown(state_ref[1])]
+    rim_start(0, vel)
+    other = [grown(jnp.exp(friction_ref[...]) * area_ref[...]), grown(beta_ref[...])]
+    rim_start(1, other)
+    vel_ref[0], vel_ref[1] = rim_finish(0, vel)
+    drag, beta = rim_finish(1, other)
+    drag_ref[...] = drag
+    for c in range(2):
+        r_ref[c] = -drag * beta * vel_ref[c]
+    stack_ref[...] = stack_field(vel_ref)
+    viscosity_loop(stack_ref, high_ref, low_ref, geom_ref, scale_ref, coef_ref, rows)
+    solve(0, 2, 0)
+    tangent_ref[...] = x_ref[:, :node_rows]
+
+    capacity = obs_high_ref.shape[1] // count
+    lines = capacity // 128
+    stack_ref[...] = stack_field(x_ref)
+
+    def read(step, carry):
+        cols = pl.ds(pl.multiple_of(step * capacity, 128), capacity)
+        _, _, values = gather_chunk(
+            stack_ref[...], obs_high_ref, obs_low_ref, cols, rows, columns
+        )
+        total = jnp.zeros((1, capacity), f32)
+        for a in range(3):
+            total = total + (
+                wx_ref[a : a + 1, cols] * values[0][a] + wy_ref[a : a + 1, cols] * values[1][a]
+            )
+        for j in range(lines):
+            pix_send[0, step, j : j + 1, :] = total[:, j * 128 : (j + 1) * 128]
+        return carry
+
+    lax.fori_loop(0, count, read, 0)
+    pix_trade(0)
+
+    dest = dest_ref[...]
+    pixel_rows = dest.shape[0]
+    named = jnp.concatenate(
+        [jnp.where(dest == q, 1.0, 0.0) for q in range(count)], axis=0
+    ).astype(jnp.bfloat16)
+    first = lax.broadcasted_iota(jnp.int32, (128, 128), 0)
+    second = lax.broadcasted_iota(jnp.int32, (128, 128), 1)
+    before = jnp.where(first < second, 1.0, 0.0).astype(jnp.bfloat16)
+    ones = jnp.ones((128, 128), jnp.bfloat16)
+    within = jnp.dot(named, before, preferred_element_type=f32)
+    per_row = jnp.dot(named, ones, preferred_element_type=f32).astype(jnp.bfloat16)
+    size = count * pixel_rows
+    first = lax.broadcasted_iota(jnp.int32, (size, size), 0)
+    second = lax.broadcasted_iota(jnp.int32, (size, size), 1)
+    start = first // pixel_rows * pixel_rows
+    above = jnp.where((second >= start) & (second < first), 1.0, 0.0).astype(jnp.bfloat16)
+    ranks = within + jnp.dot(above, per_row, preferred_element_type=f32)
+    rank = jnp.zeros((pixel_rows, 128), f32)
+    for q in range(count):
+        rank = rank + jnp.where(dest == q, ranks[q * pixel_rows : (q + 1) * pixel_rows], 0.0)
+    rank = rank.astype(jnp.int32)
+    slot_line = dest * TILE + rank // 128
+    slot_lane = lax.rem(rank, 128)
+
+    def flat(value):
+        return jnp.concatenate([value[i : i + 1] for i in range(pixel_rows)], axis=1)
+
+    table = count * TILE
+    line_mask = row_mask(flat(slot_line), table)
+    lane_hot = column_onehot(flat(slot_lane), 128)
+    high, low = split_pair(pix_recv[0].reshape(table, 128))
+    spread_out = jnp.dot(
+        jnp.concatenate([high, low], axis=0), lane_hot, preferred_element_type=f32
+    )
+    spread_out = spread_out[:table] + spread_out[table:]
+    line = jnp.sum(jnp.where(line_mask, spread_out, 0.0), axis=0, keepdims=True)
+    reading = jnp.concatenate(
+        [line[:, i * 128 : (i + 1) * 128] for i in range(pixel_rows)], axis=0
+    )
+    precision = prec_ref[...]
+    column = lax.broadcasted_iota(jnp.int32, (pixel_rows, 128), 1)
+    link = jnp.where(
+        column < 127,
+        couple_ref[...] * jnp.sqrt(precision * pltpu.roll(precision, 127, 1)),
+        0.0,
+    )
+    weighted = (
+        precision * reading
+        - link * pltpu.roll(reading, 127, 1)
+        - pltpu.roll(link, 1, 1) * pltpu.roll(reading, 1, 1)
+    )
+    weighted = flat(weighted)
+    top = weighted.astype(jnp.bfloat16).astype(f32)
+    left = jnp.concatenate(
+        [jnp.where(line_mask, part, 0.0).astype(jnp.bfloat16) for part in (top, weighted - top)],
+        axis=0,
+    )
+    out = lax.dot_general(
+        left, lane_hot, (((1,), (1,)), ((), ())), preferred_element_type=f32
+    )
+    pix_send[1] = (out[:table] + out[table:]).reshape(count, TILE, 128)
+    pix_trade(1)
+
+    total_ref[...] = jnp.zeros_like(total_ref)
+
+    def scatter(step, carry):
+        cols = pl.ds(pl.multiple_of(step * capacity, 128), capacity)
+        tile = pix_recv[1, step]
+        arrived = jnp.concatenate([tile[j : j + 1] for j in range(lines)], axis=1)
+        stacks, onehots = [], []
+        for a in range(3):
+            mask = row_mask(obs_high_ref[a : a + 1, cols], rows)
+            onehots.append(column_onehot(obs_low_ref[a : a + 1, cols], columns))
+            stacks.append(
+                masked_stack(
+                    mask, arrived * wx_ref[a : a + 1, cols], arrived * wy_ref[a : a + 1, cols]
+                )
+            )
+        total_ref[...] += add_in(stacks, onehots)
+        return carry
+
+    lax.fori_loop(0, count, scatter, 0)
+    local = core_sum(2)
+    rim_start(4, local)
+    r_ref[0], r_ref[1] = rim_finish(4, local)
+    solve(3, 5, 3)
+    hess_ref[...] = -drag_ref[:node_rows] * (
+        state_ref[0] * x_ref[0, :node_rows] + state_ref[1] * x_ref[1, :node_rows]
+    )
+
+
+def fused_device(
+    state_vel,
+    friction,
+    basal_area,
+    direction_beta,
+    elem_nodes,
+    elem_geom,
+    elem_thick,
+    live_blocks,
+    pix_dest,
+    pix_prec,
+    pix_couple,
+    obs_nodes,
+    obs_bary,
+    obs_angle,
+):
+    node_rows, columns = friction.shape
+    rows = -(-(node_rows + 3) // 8) * 8
+    elements = elem_nodes.shape[1]
+    wide, narrow = lax.axis_size("wide"), lax.axis_size("narrow")
+    count = wide * narrow
+    alive = jnp.arange(elements, dtype=jnp.int32) // 128 < live_blocks[lax.axis_index("sub")]
+    scale = jnp.where(alive, elem_thick * elem_geom[6], 0.0)[None, :]
+    high, low = node_ids(elem_nodes, node_rows, columns)
+    obs_high, obs_low = node_ids(obs_nodes, node_rows, columns)
+    weight_x = obs_bary * jnp.cos(obs_angle)
+    weight_y = obs_bary * jnp.sin(obs_angle)
+    f32 = jnp.float32
+    pair = pltpu.VMEM((2, rows, columns), f32)
+    args = (
+        state_vel,
+        friction,
+        basal_area,
+        direction_beta,
+        high,
+        low,
+        elem_geom,
+        scale,
+        pix_dest.reshape(-1, 128),
+        pix_prec.reshape(-1, 128),
+        pix_couple.reshape(-1, 128),
+        obs_high,
+        obs_low,
+        weight_x,
+        weight_y,
+    )
+    dma = pltpu.SemaphoreType.DMA
+    return pl.pallas_call(
+        functools.partial(whole_kernel, wide, narrow),
+        out_shape=(
+            jax.ShapeDtypeStruct((2, node_rows, columns), f32),
+            jax.ShapeDtypeStruct((node_rows, columns), f32),
+        ),
+        in_specs=[pl.BlockSpec(memory_space=pltpu.VMEM)] * len(args),
+        out_specs=(pl.BlockSpec(memory_space=pltpu.VMEM),) * 2,
+        scratch_shapes=[
+            pltpu.VMEM((4 * rows, columns), jnp.bfloat16),
+            pltpu.VMEM((4 * rows, columns), f32),
+            pltpu.VMEM((1, elements), f32),
+            pltpu.VMEM((rows, columns), f32),
+            pair,
+            pair,
+            pair,
+            pair,
+            pair,
+            pltpu.VMEM((5, 2, rows, columns), f32),
+            pltpu.VMEM((5, 2, rows, columns), f32),
+            pltpu.VMEM((7, 16, columns), f32),
+            pltpu.VMEM((7, 9, 16, columns), f32),
+            pltpu.VMEM((6, 8, 128), f32),
+            pltpu.VMEM((6, count, 8, 128), f32),
+            pltpu.VMEM((2, count, TILE, 128), f32),
+            pltpu.VMEM((2, count, TILE, 128), f32),
+            dma((5,)),
+            dma((5,)),
+            dma((7, 9)),
+            dma((7, 9)),
+            dma((6, count)),
+            dma((6, count)),
+            dma((2, count)),
+            dma((2, count)),
+        ],
+        compiler_params=pltpu.CompilerParams(
+            collective_id=0, has_side_effects=True, vmem_limit_bytes=48 * 1024 * 1024
+        ),
+    )(*args)
+
+
+def choose(*args):
+    count = lax.axis_size("wide") * lax.axis_size("narrow")
+    capacity = args[-1].shape[0] // count
+    columns = args[1].shape[1]
+    if capacity % 128 == 0 and capacity <= 128 * TILE and columns == 2 * RIM and args[1].shape[0] + 2 <= RIM:
+        return fused_device(*args)
+    return per_device(*args)
+
+
 def solution(mesh):
     placed = (
         P(None, ("groups", "wide"), "narrow"),
@@ -418,7 +962,7 @@
         P(("groups", "wide", "narrow", "sub")),
     )
     return jax.shard_map(
-        per_device,
+        choose,
         mesh=mesh,
         in_specs=placed,
         out_specs=(P(None, ("groups", "wide"), "narrow"), P(("groups", "wide"), "narrow")),

time: 706 us -> 134 us (0.19); the launches traced: 697 us -> 134 us
  local copies, waits for them, and re-layouts: 182 us -> 5.04 us
  waiting for transfers between devices: 170 us -> 0 us
  blocking collectives: 131 us -> 0 us
  starting transfers between devices: 105 us -> 0 us
  Pallas kernels: 69.4 us -> 127 us
  between operations: 23.5 us -> 0.77 us
  other arithmetic: 15.4 us -> 1.16 us
    scatter-add x10 -> x0, local copies, waits for them, and re-layouts: 129 us -> none  [reduce_rims(): return interior.at[:, 0].add(across[:, 0]).at[:, -1].add(across[:, 3])]
    psum x6 -> x0, blocking collectives: 122 us -> none  [the longest x4 78.6 us: norm_sum(): return lax.psum(jnp.sum(residual * residual), ('wide', 'narrow'))]
    ppermute x44 -> x0, starting transfers between devices: 102 us -> none  [the longest x22 72.9 us: padded(): lax.ppermute(lax.slice_in_dim(block, block.shape[dim] - width, None, axis...]
    psum x5 -> x0, waiting for transfers between devices: 89.4 us -> none  [finish(): both = lax.psum(partial, 'sub')]
    ppermute x44 -> x0, waiting for transfers between devices: 74.4 us -> none  [the longest x22 53.3 us: padded(): lax.ppermute(lax.slice_in_dim(block, 0, width, axis=dim), axis, backward)]
    pallas_call x7 -> x1, Pallas kernels: 69.4 us -> 127 us  [fused_device(): pl.pallas_call(functools.partial(whole_kernel, wide, narrow), out_shape=(...]
    gather x1 -> x0, local copies, waits for them, and re-layouts: 11.8 us -> none  [per_device(): returned.reshape(-1)[slot_index]]
    slice x31 -> x1, local copies, waits for them, and re-layouts: 12.5 us -> 0.96 us  [fused_device(): scale = jnp.where(alive, elem_thick * elem_geom[6], 0.0)[None, :]]
  transfers between devices with their start and end apart: 50 -> 0, of which waited for: 31 -> 0; matrix products, arithmetic and copies ran while one was open for 5% -> 0% of each run, Pallas kernels for 0% -> 0%
where the time goes in v2:
time: 134 us
  Pallas kernels  127 us (95%)
  local copies, waits for them, and re-layouts  5.04 us (4%)
    pallas_call x1, Pallas kernels, fused_device(): pl.pallas_call(functools.partial(whole_kernel, wide, narrow), out_shape=(...  127 us
    unnamed x30, local copies, waits for them, and re-layouts  3.43 us

profile of v2, /device:TPU:0, one launch (start us, length us, event | category | flops | bytes accessed | tf_op | source)
XLA Modules:
  0.0 133.9 jit_solution(16285052748146965968)
XLA Ops:
  0.6 0.0 copy-start.13
  0.6 0.6 copy-done.13
  1.3 0.6 dynamic_slice.3
  1.9 0.0 copy-start.11
  1.9 0.0 copy-start.12
  1.9 1.0 slice.3
  2.8 0.0 copy-start.9
  2.9 0.0 copy-done.11
  2.9 0.7 multiply_select_fusion
  3.6 0.0 copy-done.12
  3.6 0.1 fusion.10
  3.6 0.0 copy-done.9
  3.7 0.8 copy-done.10
  4.5 0.2 select_select_fusion.1
  4.7 0.0 copy-start
  4.7 0.0 copy-done.8
  4.7 0.0 copy-start.2
  4.7 0.0 copy-start.5
  4.8 0.0 copy-start.6
  4.8 0.0 copy-start.7
  4.8 0.3 select_select_fusion
  5.1 0.0 copy-done.4
  5.1 0.4 copy-done.1
  5.5 0.0 copy-done.3
  5.5 0.2 copy-done
  5.7 0.0 copy-done.2
  5.7 0.0 copy-done.5
  5.7 0.0 copy-done.6
  5.7 0.0 copy-done.7
  5.7 126.9 %shard_map.149 = (f32[2,64,256]{2,1,0:T(8,128)S(1)}, f32[64,256]{1,0:T(8,128)S(1)}) custom-call(f32[2,64,256]{2,1,0:T(8,128)S(1)} %copy-done.1, f32[64,256]{1,0:T(8,128)S(1)} %copy-done.2, f32[64,256]{1,0:T(8,128)S(1)} %copy-done.3, f32[64,256]{1,0:T(8,128)S(1)} %copy-done.4, s32[3,6144]{1,0:T(4,128)S(1)} %get-tuple-element.3.high_ref, ...), custom_call_target="tpu_custom_call" | custom-call | tf_op jit(solution)/shard_map/pallas_call | solution.py:897
  132.6 0.7 copy.18
  133.3 0.6 copy.19
  (6 shorter events, 0.0 us)
Async XLA Ops:
  0.6 0.7 copy-start.13
  1.9 1.0 copy-start.11
  1.9 1.7 %copy-start.12 = (f32[4096]{0:T(1024)S(1)}, f32[4096]{0:T(1024)}, u32[]{:S(2)}) copy-start(f32[4096]{0:T(1024)} %param.27) | copy-start | bytes 49156
  2.8 0.8 copy-start.9
  3.7 0.8 copy-start.10
  3.7 1.0 copy-start.8
  3.7 1.4 %copy-start.4 = (f32[64,256]{1,0:T(8,128)S(1)}, f32[64,256]{1,0:T(8,128)}, u32[]{:S(2)}) copy-start(f32[64,256]{1,0:T(8,128)} %beta_ref.1) | copy-start | bytes 196612
  4.5 0.9 copy-start.1
  4.5 0.9 copy-start.3
  4.7 1.0 copy-start
  4.7 0.9 copy-start.2
  4.7 0.9 copy-start.5
  4.8 0.9 copy-start.6
  4.8 0.9 copy-start.7

commit v3 on v2

--- a/solution.py
+++ b/solution.py
@@ -410,6 +410,66 @@
     return high, low
 
 
+SCALE = 12
+
+
+def shared_chunk(stack_ref, work_ref, cols, rows):
+    width = stack_ref.shape[1]
+    ids = work_ref[0:6, cols].astype(jnp.int32)
+    masks, onehots, value_x, value_y = [], [], [], []
+    for a in range(3):
+        masks.append(row_mask(ids[a : a + 1], rows))
+        onehots.append(column_onehot(ids[3 + a : 4 + a], width))
+        got_x, got_y = pick(stack_ref[...], masks[a], onehots[a])
+        value_x.append(got_x)
+        value_y.append(got_y)
+    grad = [work_ref[6 + i : 7 + i, cols] for i in range(6)]
+    return masks, onehots, grad, strain_rows((value_x, value_y), grad)
+
+
+def shared_viscosity(stack_ref, work_ref, coef_ref, rows):
+    def body(step, carry):
+        cols = chunk_of(step)
+        _, _, _, (exx, eyy, exy) = shared_chunk(stack_ref, work_ref, cols, rows)
+        effective = exx * exx + eyy * eyy + exx * eyy + exy * exy + STRAIN_FLOOR
+        viscosity = 0.5 * GLEN_B * jnp.exp(jnp.log(effective) * (-1.0 / 3.0))
+        coef_ref[:, cols] = 2.0 * viscosity * work_ref[SCALE : SCALE + 1, cols]
+        return carry
+
+    lax.fori_loop(0, work_ref.shape[1] // CHUNK, body, 0, unroll=2)
+
+
+def shared_operate(stack_ref, work_ref, coef_ref, total_ref, rows):
+    total_ref[...] = jnp.zeros_like(total_ref)
+
+    def body(step, carry):
+        total = total_ref[...]
+        parts = []
+        for half in range(2):
+            cols = chunk_of(2 * step + half)
+            masks, onehots, grad, strain = shared_chunk(stack_ref, work_ref, cols, rows)
+            exx, eyy, exy = strain
+            coefficient = coef_ref[:, cols]
+            sxx = coefficient * (2.0 * exx + eyy)
+            syy = coefficient * (exx + 2.0 * eyy)
+            sxy = coefficient * exy
+            stacks = [
+                masked_stack(
+                    masks[a],
+                    sxx * grad[a] + sxy * grad[3 + a],
+                    syy * grad[3 + a] + sxy * grad[a],
+                )
+                for a in range(3)
+            ]
+            parts.append((stacks, onehots))
+        for stacks, onehots in parts:
+            total = total + add_in(stacks, onehots)
+        total_ref[...] = total
+        return carry
+
+    lax.fori_loop(0, work_ref.shape[1] // (2 * CHUNK), body, 0)
+
+
 SIDES = [(dw, dn) for dw in (-1, 0, 1) for dn in (-1, 0, 1)]
 TILE = 8
 
@@ -421,10 +481,8 @@
     friction_ref,
     area_ref,
     beta_ref,
-    high_ref,
-    low_ref,
-    geom_ref,
-    scale_ref,
+    packed_ref,
+    live_ref,
     dest_ref,
     prec_ref,
     couple_ref,
@@ -451,6 +509,9 @@
     sum_recv,
     pix_send,
     pix_recv,
+    other_ref,
+    work_ref,
+    other_sems,
     field_ss,
     field_rs,
     rim_ss,
@@ -484,6 +545,15 @@
         )
     pl.semaphore_wait(barrier, count)
 
+    trade = pltpu.make_async_remote_copy(
+        src_ref=packed_ref,
+        dst_ref=other_ref,
+        send_sem=other_sems.at[0],
+        recv_sem=other_sems.at[1],
+        device_id=partner,
+        device_id_type=pl.DeviceIdType.MESH,
+    )
+    trade.start()
     row_at = lax.broadcasted_iota(jnp.int32, (rows, columns), 0)
     lane_at = lax.broadcasted_iota(jnp.int32, (rows, columns), 1)
     eye_row = lax.broadcasted_iota(jnp.int32, (rows, RIM), 0)
@@ -684,7 +754,7 @@
         norm_now = None
         for step in range(CG_ITERS):
             stack_ref[...] = stack_field(p_ref)
-            operate_loop(stack_ref, high_ref, low_ref, geom_ref, coef_ref, total_ref, rows)
+            shared_operate(stack_ref, work_ref, coef_ref, total_ref, rows)
             local = core_sum(field_at + step)
             rim_start(rim_at + step, local)
             energy = dot(local[0], p_ref[0]) + dot(local[1], p_ref[1])
@@ -731,7 +801,28 @@
     for c in range(2):
         r_ref[c] = -drag * beta * vel_ref[c]
     stack_ref[...] = stack_field(vel_ref)
-    viscosity_loop(stack_ref, high_ref, low_ref, geom_ref, scale_ref, coef_ref, rows)
+    trade.wait()
+    share = work_ref.shape[1] // 128
+    blocks = packed_ref.shape[0]
+    first_live = live_ref[0]
+    all_live = first_live + live_ref[1]
+
+    def take(i, carry):
+        position = my_s * share + i
+        of_first = position < first_live
+        at = jnp.where(
+            of_first, jnp.minimum(position, blocks - 1), jnp.clip(position - first_live, 0, blocks - 1)
+        )
+        mine = jnp.where(of_first, 1, 0) + my_s == 1
+        block = jnp.where(mine, packed_ref[at], other_ref[at])
+        alive = (position < all_live) | (piece_row < SCALE)
+        cols = pl.ds(pl.multiple_of(i * 128, 128), 128)
+        work_ref[:, cols] = jnp.where(alive, block, 0.0)
+        return carry
+
+    piece_row = lax.broadcasted_iota(jnp.int32, (16, 128), 0)
+    lax.fori_loop(0, share, take, 0)
+    shared_viscosity(stack_ref, work_ref, coef_ref, rows)
     solve(0, 2, 0)
     tangent_ref[...] = x_ref[:, :node_rows]
 
@@ -753,7 +844,7 @@
             pix_send[0, step, j : j + 1, :] = total[:, j * 128 : (j + 1) * 128]
         return carry
 
-    lax.fori_loop(0, count, read, 0)
+    lax.fori_loop(0, count, read, 0, unroll=2)
     pix_trade(0)
 
     dest = dest_ref[...]
@@ -837,7 +928,7 @@
         total_ref[...] += add_in(stacks, onehots)
         return carry
 
-    lax.fori_loop(0, count, scatter, 0)
+    lax.fori_loop(0, count, scatter, 0, unroll=2)
     local = core_sum(2)
     rim_start(4, local)
     r_ref[0], r_ref[1] = rim_finish(4, local)
@@ -871,6 +962,18 @@
     alive = jnp.arange(elements, dtype=jnp.int32) // 128 < live_blocks[lax.axis_index("sub")]
     scale = jnp.where(alive, elem_thick * elem_geom[6], 0.0)[None, :]
     high, low = node_ids(elem_nodes, node_rows, columns)
+    packed = jnp.concatenate(
+        [
+            high.astype(jnp.float32),
+            low.astype(jnp.float32),
+            elem_geom[0:6],
+            scale,
+            jnp.zeros((3, elements), jnp.float32),
+        ],
+        axis=0,
+    )
+    packed = packed.reshape(16, -1, 128).transpose(1, 0, 2)
+    share = 2 * (elements // 128) // 3
     obs_high, obs_low = node_ids(obs_nodes, node_rows, columns)
     weight_x = obs_bary * jnp.cos(obs_angle)
     weight_y = obs_bary * jnp.sin(obs_angle)
@@ -881,10 +984,8 @@
         friction,
         basal_area,
         direction_beta,
-        high,
-        low,
-        elem_geom,
-        scale,
+        packed,
+        live_blocks,
         pix_dest.reshape(-1, 128),
         pix_prec.reshape(-1, 128),
         pix_couple.reshape(-1, 128),
@@ -900,12 +1001,15 @@
             jax.ShapeDtypeStruct((2, node_rows, columns), f32),
             jax.ShapeDtypeStruct((node_rows, columns), f32),
         ),
-        in_specs=[pl.BlockSpec(memory_space=pltpu.VMEM)] * len(args),
+        in_specs=[
+            pl.BlockSpec(memory_space=pltpu.SMEM if arg is live_blocks else pltpu.VMEM)
+            for arg in args
+        ],
         out_specs=(pl.BlockSpec(memory_space=pltpu.VMEM),) * 2,
         scratch_shapes=[
             pltpu.VMEM((4 * rows, columns), jnp.bfloat16),
             pltpu.VMEM((4 * rows, columns), f32),
-            pltpu.VMEM((1, elements), f32),
+            pltpu.VMEM((1, share * 128), f32),
             pltpu.VMEM((rows, columns), f32),
             pair,
             pair,
@@ -920,6 +1024,9 @@
             pltpu.VMEM((6, count, 8, 128), f32),
             pltpu.VMEM((2, count, TILE, 128), f32),
             pltpu.VMEM((2, count, TILE, 128), f32),
+            pltpu.VMEM(packed.shape, f32),
+            pltpu.VMEM((16, share * 128), f32),
+            dma((2,)),
             dma((5,)),
             dma((5,)),
             dma((7, 9)),
@@ -939,7 +1046,9 @@
     count = lax.axis_size("wide") * lax.axis_size("narrow")
     capacity = args[-1].shape[0] // count
     columns = args[1].shape[1]
-    if capacity % 128 == 0 and capacity <= 128 * TILE and columns == 2 * RIM and args[1].shape[0] + 2 <= RIM:
+    share = 2 * (args[4].shape[1] // 128) // 3
+    fits = share * 128 % (2 * CHUNK) == 0 and count % 2 == 0
+    if fits and capacity % 128 == 0 and capacity <= 128 * TILE and columns == 2 * RIM and args[1].shape[0] + 2 <= RIM:
         return fused_device(*args)
     return per_device(*args)
 

time: 134 us -> 108 us (0.81)
  Pallas kernels: 127 us -> 99 us
    pallas_call x1, Pallas kernels: 127 us -> 99 us  [fused_device(): pl.pallas_call(functools.partial(whole_kernel, wide, narrow), out_shape=(...]
    unnamed x30 -> x28, local copies, waits for them, and re-layouts: 3.43 us -> 3.66 us
where the time goes in v3:
time: 108 us
  Pallas kernels  99 us (92%)
  local copies, waits for them, and re-layouts  5.78 us (5%)
  other arithmetic  1.92 us (2%)
    pallas_call x1, Pallas kernels, fused_device(): pl.pallas_call(functools.partial(whole_kernel, wide, narrow), out_shape=(...  99 us
    unnamed x28, local copies, waits for them, and re-layouts  3.66 us

profile of v3, /device:TPU:0, one launch (start us, length us, event | category | flops | bytes accessed | tf_op | source)
XLA Modules:
  0.0 107.5 jit_solution(11501839483189426685)
XLA Ops:
  0.6 0.0 copy-start.7
  0.6 0.0 copy-start.9
  0.7 0.6 copy-done.7
  1.3 0.6 dynamic_slice.3
  1.9 1.0 slice.7
  2.8 0.0 copy-start.8
  2.8 1.4 %multiply_select_fusion = f32[6144]{0:T(1024)S(1)} fusion(f32[6144]{0:T(1024)} %param.20, f32[6144]{0:T(1024)S(1)} %bitcast.17, s32[]{:T(128)} %bitcast.3), kind=kLoop, calls=%fused_computation.34 | loop fusion | flops 67584 | bytes 73732 | tf_op jit(solution)/shard_map/jit(_where)/select_n | solution.py:963
  4.3 0.0 copy-done.9
  4.3 0.3 convert_bitcast_fusion
  4.6 0.0 copy-done.8
  4.6 0.0 copy-start.12
  4.6 0.0 copy-start.10
  4.6 0.5 concatenate.16
  5.1 0.2 copy-done.12
  5.3 0.1 fusion.12
  5.4 0.1 copy-done.10
  5.5 0.0 copy-start.11
  5.5 0.0 copy-start.6
  5.5 0.0 copy-start
  5.6 0.8 copy-done.11
  6.3 0.2 select_select_fusion
  6.5 0.0 copy-start.4
  6.5 0.0 copy-done.2
  6.5 0.0 copy-done.3
  6.5 0.0 copy-done.5
  6.5 0.0 copy-done.6
  6.6 0.0 copy-done
  6.6 0.6 copy-done.1
  7.2 0.0 copy-done.4
  7.2 99.0 %shard_map.149 = (f32[2,64,256]{2,1,0:T(8,128)S(1)}, f32[64,256]{1,0:T(8,128)S(1)}) custom-call(f32[2,64,256]{2,1,0:T(8,128)S(1)} %copy-done, f32[64,256]{1,0:T(8,128)S(1)} %copy-done.1, f32[64,256]{1,0:T(8,128)S(1)} %copy-done.2, f32[64,256]{1,0:T(8,128)S(1)} %copy-done.3, f32[48,16,128]{2,1,0:T(8,128)S(1)} %bitcast.13, s32[2]{0:T(128)S(1)} %copy-done.7, ...), custom_call_target="tpu_custom_call" | custom-call | tf_op jit(solution)/shard_map/pallas_call | solution.py:998
  106.2 0.7 copy.18
  106.9 0.6 copy.19
  (7 shorter events, 0.1 us)
Async XLA Ops:
  0.6 0.7 copy-start.7
  0.6 3.6 %copy-start.9 = (s32[3,6144]{1,0:T(4,128)S(1)}, s32[3,6144]{1,0:T(4,128)}, u32[]{:S(2)}) copy-start(s32[3,6144]{1,0:T(4,128)} %param.18) | copy-start | bytes 221188
  2.8 1.7 %copy-start.8 = (f32[7,6144]{1,0:T(8,128)S(1)}, f32[7,6144]{1,0:T(8,128)}, u32[]{:S(2)}) copy-start(f32[7,6144]{1,0:T(8,128)} %param.19) | copy-start | bytes 516100
  4.6 0.7 copy-start.12
  4.6 0.8 copy-start.10
  5.5 0.8 copy-start.11
  5.5 1.0 copy-start.2
  5.5 1.0 copy-start.3
  5.5 1.1 copy-start.5
  5.5 1.1 copy-start.6
  5.5 1.0 copy-start
  6.3 0.9 copy-start.1
  6.5 0.7 copy-start.4

commit v4 on v3

--- a/solution.py
+++ b/solution.py
@@ -716,18 +716,20 @@
             total = total + sum_recv[k, q]
         return total[0:1, 0:1], total[1:2, 0:1]
 
-    def pix_trade(k):
+    def pix_start(k):
         for j in range(1, count):
             q = lax.rem(me + j, count)
             all_copy(pix_send.at[k, q], pix_recv, pix_ss, pix_rs, k, q, me).start()
         pix_recv[k, me] = pix_send[k, me]
+
+    def pix_finish(k):
         for j in range(1, count):
             q = lax.rem(me + j, count)
             copy = all_copy(pix_send.at[k, q], pix_recv, pix_ss, pix_rs, k, q, q)
             copy.wait_recv()
             copy.wait_send()
 
-    def core_sum(k):
+    def core_start(k):
         field_send[k, 0], field_send[k, 1] = unstack(total_ref[...])
         copy = pltpu.make_async_remote_copy(
             src_ref=field_send.at[k],
@@ -738,6 +740,9 @@
             device_id_type=pl.DeviceIdType.MESH,
         )
         copy.start()
+        return copy
+
+    def core_finish(k, copy):
         copy.wait()
         return [field_send[k, c] + field_recv[k, c] for c in range(2)]
 
@@ -755,29 +760,32 @@
         for step in range(CG_ITERS):
             stack_ref[...] = stack_field(p_ref)
             shared_operate(stack_ref, work_ref, coef_ref, total_ref, rows)
-            local = core_sum(field_at + step)
-            rim_start(rim_at + step, local)
-            energy = dot(local[0], p_ref[0]) + dot(local[1], p_ref[1])
+            copy = core_start(field_at + step)
+            norm = both(r_ref, r_ref, node_rows)
+            energy = jnp.zeros((1, 1), f32)
             for c in range(2):
                 field = p_ref[c, :node_rows]
                 energy = energy + dot(drag_ref[:node_rows] * field, field)
-            norm = both(r_ref, r_ref, node_rows)
+            local = core_finish(field_at + step, copy)
+            rim_start(rim_at + step, local)
+            energy = energy + dot(local[0], p_ref[0]) + dot(local[1], p_ref[1])
             sum_start(sum_at + 2 * step, norm, energy)
             applied = rim_finish(rim_at + step, local)
             for c in range(2):
                 q_ref[c] = applied[c] + drag_ref[...] * p_ref[c]
             norm_now, energy = sum_finish(sum_at + 2 * step)
             alpha = norm_now / energy
+            if step + 1 < CG_ITERS:
+                for c in range(2):
+                    r_ref[c] = r_ref[c] - alpha * q_ref[c]
+                norm = both(r_ref, r_ref, node_rows)
+                sum_start(sum_at + 2 * step + 1, norm)
             for c in range(2):
                 if step == 0:
                     x_ref[c] = alpha * p_ref[c]
                 else:
                     x_ref[c] = x_ref[c] + alpha * p_ref[c]
             if step + 1 < CG_ITERS:
-                for c in range(2):
-                    r_ref[c] = r_ref[c] - alpha * q_ref[c]
-                norm = both(r_ref, r_ref, node_rows)
-                sum_start(sum_at + 2 * step + 1, norm)
                 norm_next, _ = sum_finish(sum_at + 2 * step + 1)
                 ratio = norm_next / norm_now
                 for c in range(2):
@@ -845,7 +853,7 @@
         return carry
 
     lax.fori_loop(0, count, read, 0, unroll=2)
-    pix_trade(0)
+    pix_start(0)
 
     dest = dest_ref[...]
     pixel_rows = dest.shape[0]
@@ -877,6 +885,7 @@
     table = count * TILE
     line_mask = row_mask(flat(slot_line), table)
     lane_hot = column_onehot(flat(slot_lane), 128)
+    pix_finish(0)
     high, low = split_pair(pix_recv[0].reshape(table, 128))
     spread_out = jnp.dot(
         jnp.concatenate([high, low], axis=0), lane_hot, preferred_element_type=f32
@@ -908,7 +917,8 @@
         left, lane_hot, (((1,), (1,)), ((), ())), preferred_element_type=f32
     )
     pix_send[1] = (out[:table] + out[table:]).reshape(count, TILE, 128)
-    pix_trade(1)
+    pix_start(1)
+    pix_finish(1)
 
     total_ref[...] = jnp.zeros_like(total_ref)
 
@@ -929,7 +939,7 @@
         return carry
 
     lax.fori_loop(0, count, scatter, 0, unroll=2)
-    local = core_sum(2)
+    local = core_finish(2, core_start(2))
     rim_start(4, local)
     r_ref[0], r_ref[1] = rim_finish(4, local)
     solve(3, 5, 3)

time: 108 us -> 108 us (level)
  no operation moved by 1% of the time
where the time goes in v4:
time: 108 us; the launch traced here: 107 us
  Pallas kernels  98.7 us (91%)
  local copies, waits for them, and re-layouts  5.78 us (5%)
  other arithmetic  1.92 us (2%)
    pallas_call x1, Pallas kernels, fused_device(): pl.pallas_call(functools.partial(whole_kernel, wide, narrow), out_shape=(...  98.7 us
    unnamed x28, local copies, waits for them, and re-layouts  3.66 us

profile of v4, /device:TPU:0, one launch (start us, length us, event | category | flops | bytes accessed | tf_op | source)
XLA Modules:
  0.0 107.2 jit_solution(2916019953881799184)
XLA Ops:
  0.6 0.0 copy-start.7
  0.6 0.0 copy-start.9
  0.7 0.6 copy-done.7
  1.3 0.6 dynamic_slice.3
  1.9 1.0 slice.7
  2.8 0.0 copy-start.8
  2.8 1.4 %multiply_select_fusion = f32[6144]{0:T(1024)S(1)} fusion(f32[6144]{0:T(1024)} %param.20, f32[6144]{0:T(1024)S(1)} %bitcast.17, s32[]{:T(128)} %bitcast.3), kind=kLoop, calls=%fused_computation.34 | loop fusion | flops 67584 | bytes 73732 | tf_op jit(solution)/shard_map/jit(_where)/select_n | solution.py:973
  4.3 0.0 copy-done.9
  4.3 0.3 convert_bitcast_fusion
  4.6 0.0 copy-done.8
  4.6 0.0 copy-start.12
  4.6 0.0 copy-start.10
  4.6 0.5 concatenate.16
  5.1 0.2 copy-done.12
  5.3 0.1 fusion.12
  5.4 0.1 copy-done.10
  5.5 0.0 copy-start.11
  5.5 0.0 copy-start.6
  5.5 0.0 copy-start
  5.6 0.8 copy-done.11
  6.3 0.2 select_select_fusion
  6.5 0.0 copy-start.4
  6.5 0.0 copy-done.2
  6.5 0.0 copy-done.3
  6.5 0.0 copy-done.5
  6.5 0.0 copy-done.6
  6.6 0.0 copy-done
  6.6 0.6 copy-done.1
  7.2 0.0 copy-done.4
  7.2 98.7 %shard_map.149 = (f32[2,64,256]{2,1,0:T(8,128)S(1)}, f32[64,256]{1,0:T(8,128)S(1)}) custom-call(f32[2,64,256]{2,1,0:T(8,128)S(1)} %copy-done, f32[64,256]{1,0:T(8,128)S(1)} %copy-done.1, f32[64,256]{1,0:T(8,128)S(1)} %copy-done.2, f32[64,256]{1,0:T(8,128)S(1)} %copy-done.3, f32[48,16,128]{2,1,0:T(8,128)S(1)} %bitcast.13, s32[2]{0:T(128)S(1)} %copy-done.7, ...), custom_call_target="tpu_custom_call" | custom-call | tf_op jit(solution)/shard_map/pallas_call | solution.py:1008
  105.9 0.7 copy.18
  106.6 0.6 copy.19
  (7 shorter events, 0.1 us)
Async XLA Ops:
  0.6 0.7 copy-start.7
  0.6 3.6 %copy-start.9 = (s32[3,6144]{1,0:T(4,128)S(1)}, s32[3,6144]{1,0:T(4,128)}, u32[]{:S(2)}) copy-start(s32[3,6144]{1,0:T(4,128)} %param.18) | copy-start | bytes 221188
  2.8 1.7 %copy-start.8 = (f32[7,6144]{1,0:T(8,128)S(1)}, f32[7,6144]{1,0:T(8,128)}, u32[]{:S(2)}) copy-start(f32[7,6144]{1,0:T(8,128)} %param.19) | copy-start | bytes 516100
  4.6 0.7 copy-start.12
  4.6 0.8 copy-start.10
  5.5 0.8 copy-start.11
  5.5 1.0 copy-start.2
  5.5 1.0 copy-start.3
  5.5 1.1 copy-start.5
  5.5 1.1 copy-start.6
  5.5 1.0 copy-start
  6.3 0.9 copy-start.1
  6.5 0.7 copy-start.4
